TPU v7x, 512 devices: a whole 4x4x16 slice. The times are simulated.
512 devices in a mesh: win: 16 (over x, y), tile: 32 (over z, core).
Axes of the slice: x: 4, y: 4, z: 16, core: 2. Of those that a mesh axis runs over, the one named last changes fastest.
Arguments:
- multiplier: float32 [16, 72, 256, 128], P('win', None, 'tile'), may hold values from -6 to 6
- coef_diag: float32 [16, 72, 256, 128], P('win', None, 'tile'), may hold values from 0.2 to 0.6
- coef_side: float32 [16, 72, 256, 128], P('win', None, 'tile'), may hold values from 0.05 to 0.15
- mixing: float32 [72, 72], replicated, may hold values from -0.75 to 0.75
- jacobians: bfloat16 [8, 72, 128], replicated, may hold values from -0.5 to 0.5
- departures: bfloat16 [16, 2, 65536, 128], P('win', None, 'tile'), may hold values from -6 to 6
- counts: int32 [16, 2, 32, 32], P('win', None, 'tile'), may hold values from 0 to 128, as said below
- row_order: int32 [16, 2, 32, 2048], P('win', None, 'tile'), may hold values from 0 to 2047, each once within a row
- obs_cell: int32 [16, 2, 65536], P('win', None, 'tile'), may hold values from 0 to 1023
- obs_block: int32 [16, 2, 65536], P('win', None, 'tile'), may hold values from 0 to 7
Outputs:
- state_adjoint: float32 [16, 72, 256, 128], P('win', None, 'tile')
Inputs may be any that keep to these rules, and one draw needn't show every extreme that they name: Each owner's counts at one time sum to at most 2048; in every sub-window and time some tile receives 128 rows from every owner.
All inputs are finite; a program needn't handle non-finite values.
Results may differ from a plain program's by a relative error of at most 0.0022.
Values may be sent and summed in bfloat16 or wider, within the bound.
No kernel may reach another device: no remote copies, remote signals or barrier semaphores. Data moves between devices by JAX's collectives and lax.ppermute only.
A program may use at most 64 MiB of HBM per device.

v0:
```python
import jax
import jax.numpy as jnp
from jax import lax
from jax.sharding import PartitionSpec as P

CAP = 128


def padded_2(array, sides, width):
    for axis, dim in sides:
        count, length = (lax.axis_size(axis), array.shape[dim])
        up = [(i, (i + 1) % count) for i in range(count)]
        down = [(j, i) for i, j in up]
        last = lax.slice_in_dim(array, length - width, length, axis=dim)
        initial = lax.slice_in_dim(array, 0, width, axis=dim)
        before = lax.ppermute(last, axis, up)
        after = lax.ppermute(initial, axis, down)
        array = jnp.concatenate([before, array, after], axis=dim)
    return array


def from_behind(array, axis, by):
    count = lax.axis_size(axis)
    pairs = [(i, i + by) for i in range(count) if 0 <= i + by < count]
    return lax.ppermute(array, axis, pairs)


def mix_channels(state_in, mixing):
    return jnp.einsum("cd,ncxy->ndxy", mixing, state_in, precision=lax.Precision.HIGHEST)


def apply_rimmed(extended, diagonal, side_coef):
    interior = extended[:, :, 1:-1, :]
    padded = jnp.pad(interior, ((0, 0), (0, 0), (0, 0), (1, 1)))
    beside = (
        extended[:, :, 2:, :] + extended[:, :, :-2, :] + padded[:, :, :, 2:] + padded[:, :, :, :-2]
    )
    return diagonal * interior + side_coef * beside


def adjoint_single(state_in, diagonal, side_coef, mixing):
    mixed = mix_channels(state_in, mixing)
    extended = padded_2(mixed, (("tile", 2),), 1)
    return apply_rimmed(extended, diagonal, side_coef)


def jacobian_rows(row_vals, block_ids, jacobians):
    summed = jnp.zeros((jacobians.shape[1], row_vals.shape[0]), jnp.float32)
    for block in range(jacobians.shape[0]):
        product = lax.dot_general(
            jacobians[block], row_vals, (((1,), (1,)), ((), ())), preferred_element_type=jnp.float32
        )
        summed = jnp.where(block_ids[None, :] == block, product, summed)
    return summed.astype(jnp.bfloat16)


def select_rows(table, wanted, precision):
    slot_count = wanted.shape[0]
    block_rows = 512
    targets = lax.iota(jnp.int32, table.shape[0])

    def select_block(block_ids):
        onehot = (block_ids[:, None] == targets[None, :]).astype(table.dtype)
        return jnp.dot(onehot, table, preferred_element_type=jnp.float32, precision=precision)

    picked = lax.map(select_block, wanted.reshape(slot_count // block_rows, block_rows))
    return picked.reshape(slot_count, table.shape[1])


def scatter_cells(values, cell_ids, cell_count):
    width = values.shape[0]
    row_count = values.shape[1]
    block_rows = 512
    block_count = row_count // block_rows
    value_blocks = values.reshape(width, block_count, block_rows).transpose(1, 0, 2)
    cell_blocks = cell_ids.reshape(block_count, block_rows)
    targets = lax.iota(jnp.int32, cell_count)

    def add_block(summed, block_in):
        block_vals, block_cells = block_in
        onehot = (block_cells[:, None] == targets[None, :]).astype(jnp.bfloat16)
        return (summed + jnp.dot(block_vals, onehot, preferred_element_type=jnp.float32), None)

    summed, _ = lax.scan(
        add_block, jnp.zeros((width, cell_count), jnp.float32), (value_blocks, cell_blocks)
    )
    return summed


def local(
    multiplier,
    coef_diag,
    coef_side,
    mixing,
    jacobians,
    departures,
    counts,
    row_order,
    obs_cell,
    obs_block,
):
    tiles = lax.axis_size("tile")
    block_kinds = jacobians.shape[0]
    channels = departures.shape[3]
    width = multiplier.shape[1]
    lon_dev = multiplier.shape[2]
    lat_rows = multiplier.shape[3]
    cell_count = lon_dev * lat_rows
    capacity = CAP
    tile_counts = counts[0, :, 0, :]
    row_ends = jnp.cumsum(tile_counts, axis=1)
    starts = row_ends - tile_counts
    slot_ids = lax.iota(jnp.int32, capacity)
    is_live = slot_ids[None, None, :] < tile_counts[:, :, None]
    padded_order = jnp.concatenate(
        [row_order[0, :, 0], jnp.zeros((2, capacity), jnp.int32)], axis=1
    )

    def tile_rows(tile_starts):
        return jnp.stack(
            [
                lax.dynamic_slice_in_dim(padded_order[moment], tile_starts[moment], capacity, 0)
                for moment in range(2)
            ]
        )

    row_ids = lax.map(tile_rows, starts.T).transpose(1, 0, 2)
    meta_all = (obs_cell[0] * block_kinds + obs_block[0]).astype(jnp.float32)
    meta_pick = jnp.stack(
        [
            select_rows(
                meta_all[moment][:, None], row_ids[moment].reshape(-1), lax.Precision.HIGHEST
            ).reshape(tiles, capacity)
            for moment in range(2)
        ]
    )
    meta_out = jnp.where(is_live, meta_pick, 0.0).astype(jnp.int32)
    meta_in = lax.all_to_all(meta_out, "tile", split_axis=1, concat_axis=1, tiled=True)
    adj_terms = []
    picked = jnp.stack(
        [
            select_rows(departures[0, moment], row_ids[moment].reshape(-1), None)
            .astype(jnp.bfloat16)
            .reshape(tiles, capacity, channels)
            for moment in range(2)
        ]
    )
    picked = jnp.where(is_live[..., None], picked, jnp.zeros((), jnp.bfloat16))
    received = lax.all_to_all(picked, "tile", split_axis=1, concat_axis=1, tiled=True)
    for moment in range(2):
        meta_flat = meta_in[moment].reshape(-1)
        values = jacobian_rows(
            received[moment].reshape(-1, channels), meta_flat % block_kinds, jacobians
        )
        adj_terms.append(scatter_cells(values, meta_flat // block_kinds, cell_count))
    adj_obs = [term.reshape(1, width, lon_dev, lat_rows) for term in adj_terms]
    following = from_behind(multiplier.astype(jnp.bfloat16), "win", -1).astype(multiplier.dtype)
    first_step = adjoint_single(following, coef_diag, coef_side, mixing)
    second = adjoint_single(adj_obs[1] - first_step, coef_diag, coef_side, mixing)
    return multiplier + adj_obs[0] + second


def solution(mesh):
    in_specs = (
        P("win", None, "tile", None),
        P("win", None, "tile", None),
        P("win", None, "tile", None),
        P(),
        P(),
        P("win", None, "tile", None),
        P("win", None, "tile", None),
        P("win", None, "tile", None),
        P("win", None, "tile"),
        P("win", None, "tile"),
    )
    out_specs = P("win", None, "tile", None)
    return jax.shard_map(local, mesh=mesh, in_specs=in_specs, out_specs=out_specs, check_vma=False)
```

profile of v0, /device:TPU:1, one launch (start us, length us, event | category | flops | bytes accessed | tf_op | source)
XLA Modules:
  0.0 382.1 jit_solution(6076708061539666207)
XLA Ops:
  3.1 149.8 %while.76 = (s32[]{:T(128)}, s32[32,2,128]{2,1,0:T(2,128)S(1)}, s32[2,2176]{1,0:T(2,128)S(1)}, s32[32,2]{0,1:T(2,128)S(1)}, s32[]{:T(128)}, /*index=5*/s32[]{:T(128)}, s32[]{:T(128)}) while((s32[]{:T(128)}, s32[32,2,128]{2,1,0:T(2,128)S(1)}, s32[2,2176]{1,0:T(2,128)S(1)}, s32[32,2]{0,1:T(2,128)S(1)}, s32[]{:T(128)}, /*index=5*/s32[]{:T(128)}, ...), condition=%wide.region_2.3_spmd, body=%wide.region_1.2_spmd.sunk | while | flops 264 | bytes 39105 | solution.py:127
  153.8 16.3 %while.77 = (s32[]{:T(128)}, f32[8,512,1]{1,2,0:T(1,128)S(1)}, s32[8,512]{1,0:T(8,128)S(1)}, f32[2048,1]{0,1:T(1,128)S(1)}, s32[]{:T(128)}) while((s32[]{:T(128)}, f32[8,512,1]{1,2,0:T(1,128)S(1)}, s32[8,512]{1,0:T(8,128)S(1)}, f32[2048,1]{0,1:T(1,128)S(1)}, s32[]{:T(128)}) %tuple.160), condition=%wide.region_4.5_spmd.clone, body=%wide.region_3.4_spmd.clone.sunk | while | flops 13631490 | bytes 16453 | solution.py:66
  153.8 2.0 fusion.176
  155.9 2.0 fusion.176
  157.9 2.0 fusion.176
  159.9 2.0 fusion.176
  162.0 2.0 fusion.176
  164.0 2.0 fusion.176
  166.0 2.0 fusion.176
  168.1 2.0 fusion.176
  170.1 16.3 %while.78 = (s32[]{:T(128)}, f32[8,512,1]{1,2,0:T(1,128)S(1)}, s32[8,512]{1,0:T(8,128)S(1)}, f32[2048,1]{0,1:T(1,128)S(1)}, s32[]{:T(128)}) while((s32[]{:T(128)}, f32[8,512,1]{1,2,0:T(1,128)S(1)}, s32[8,512]{1,0:T(8,128)S(1)}, f32[2048,1]{0,1:T(1,128)S(1)}, s32[]{:T(128)}) %tuple.157), condition=%wide.region_6.7_spmd.clone, body=%wide.region_5.6_spmd.clone.sunk | while | flops 13631490 | bytes 16453 | solution.py:66
  170.2 2.0 fusion.178
  172.2 2.0 fusion.178
  174.3 2.0 fusion.178
  176.3 2.0 fusion.178
  178.3 2.0 fusion.178
  180.4 2.0 fusion.178
  182.4 2.0 fusion.178
  184.4 2.0 fusion.178
  187.2 16.7 %all-to-all-start = ((s32[2,32,128]{2,0,1:T(2,128)}), s32[2,32,128]{2,0,1:T(2,128)S(1)}, u32[]{:S(2)}, u32[]{:S(2)}) async-start(s32[2,32,128]{2,0,1:T(2,128)} %fusion.79), calls=%async_computation | async-start | bytes 65536 | tf_op jit(solution)/shard_map/all_to_all | solution.py:138
  204.3 7.5 %while.79 = (s32[]{:T(128)}, bf16[8,512,128]{2,1,0:T(8,128)(2,1)S(1)}, s32[8,512]{1,0:T(8,128)S(1)}, bf16[2048,128]{1,0:T(8,128)(2,1)S(1)}, s32[]{:T(128)}) while((s32[]{:T(128)}, bf16[8,512,128]{2,1,0:T(8,128)(2,1)S(1)}, s32[8,512]{1,0:T(8,128)S(1)}, bf16[2048,128]{1,0:T(8,128)(2,1)S(1)}, s32[]{:T(128)}) %tuple.172), condition=%wide.region_8.9_spmd.clone, body=%wide.region_7.8_spmd.clone.sunk | while | flops 269484032 | bytes 792645 | solution.py:66
  211.9 7.5 %while.80 = (s32[]{:T(128)}, bf16[8,512,128]{2,1,0:T(8,128)(2,1)S(1)}, s32[8,512]{1,0:T(8,128)S(1)}, bf16[2048,128]{1,0:T(8,128)(2,1)S(1)}, s32[]{:T(128)}) while((s32[]{:T(128)}, bf16[8,512,128]{2,1,0:T(8,128)(2,1)S(1)}, s32[8,512]{1,0:T(8,128)S(1)}, bf16[2048,128]{1,0:T(8,128)(2,1)S(1)}, s32[]{:T(128)}) %tuple.173), condition=%wide.region_10.11_spmd.clone, body=%wide.region_9.10_spmd.clone.sunk | while | flops 269484032 | bytes 792645 | solution.py:66
  219.4 2.6 maximum_select_fusion
  222.0 12.3 %all-to-all-start.1 = ((bf16[2,32,128,128]{3,2,0,1:T(8,128)(2,1)}), bf16[2,32,128,128]{3,2,0,1:T(8,128)(2,1)S(1)}, u32[]{:S(2)}, u32[]{:S(2)}) async-start(bf16[2,32,128,128]{3,2,0,1:T(8,128)(2,1)} %maximum_select_fusion), calls=%async_computation.1 | async-start | bytes 4194304 | tf_op jit(solution)/shard_map/all_to_all | solution.py:149
  234.4 1.5 collective-permute-start
  237.3 4.2 %collective-permute-done = bf16[1,72,8,128]{3,1,2,0:T(8,128)(2,1)S(1)} collective-permute-done((bf16[1,72,8,128]{3,1,2,0:T(8,128)(2,1)S(1)}, bf16[1,72,8,128]{3,1,2,0:T(8,128)(2,1)S(1)}, u32[]{:S(2)}, u32[]{:S(2)}) %collective-permute-start) | collective-permute-done | bytes 147488 | tf_op jit(solution)/shard_map/ppermute | solution.py:25
  242.5 1.0 collective-permute-start.1
  243.5 1.3 collective-permute-start.2
  244.8 88.0 %all-to-all-done.1 = bf16[2,32,128,128]{3,2,0,1:T(8,128)(2,1)S(1)} async-done(((bf16[2,32,128,128]{3,2,0,1:T(8,128)(2,1)}), bf16[2,32,128,128]{3,2,0,1:T(8,128)(2,1)S(1)}, u32[]{:S(2)}, u32[]{:S(2)}) %all-to-all-start.1) | async-done | bytes 2097184 | tf_op jit(solution)/shard_map/all_to_all | solution.py:149
  333.0 1.5 fusion.84
  334.5 2.3 fusion.88
  336.9 1.6 fusion.92
  338.5 1.6 fusion.96
  346.3 0.9 fusion.44
  348.9 18.4 %while.82 = (s32[]{:T(128)}, f32[72,1024]{1,0:T(8,128)}, bf16[8,72,512]{2,1,0:T(8,128)(2,1)}, s32[8,512]{1,0:T(8,128)S(1)}, s32[]{:T(128)}, /*index=5*/s32[]{:T(128)}) while((s32[]{:T(128)}, f32[72,1024]{1,0:T(8,128)}, bf16[8,72,512]{2,1,0:T(8,128)(2,1)}, s32[8,512]{1,0:T(8,128)S(1)}, s32[]{:T(128)}, ...), condition=%wide.region_14.15_spmd.clone, body=%wide.region_13.14_spmd.clone.sunk | while | flops 76169216 | bytes 670291 | solution.py:84
  349.0 2.2 fusion.186
  351.2 2.3 fusion.186
  353.5 2.3 fusion.186
  355.8 2.3 fusion.186
  358.1 2.3 fusion.186
  360.4 2.3 fusion.186
  362.7 2.3 fusion.186
  365.0 2.3 fusion.186
  367.4 2.4 fusion.50
  370.9 1.5 convolution_bitcast_fusion
  372.4 1.3 collective-permute-start.3
  373.7 2.0 collective-permute-start.4
  375.7 5.2 %while.81 = (s32[]{:T(128)}, f32[72,1024]{1,0:T(8,128)S(1)}, bf16[8,72,512]{2,1,0:T(8,128)(2,1)S(1)}, s32[8,512]{1,0:T(8,128)S(1)}, s32[]{:T(128)}, /*index=5*/s32[]{:T(128)}) while((s32[]{:T(128)}, f32[72,1024]{1,0:T(8,128)S(1)}, bf16[8,72,512]{2,1,0:T(8,128)(2,1)S(1)}, s32[8,512]{1,0:T(8,128)S(1)}, s32[]{:T(128)}, ...), condition=%wide.region_12.13_spmd.clone, body=%wide.region_11.12_spmd.clone.sunk | while | flops 76169216 | bytes 669783 | solution.py:84
  (331 shorter events, 62.1 us)
Async XLA Ops:
  0.0 241.5 %copy-start = (f32[72,72]{1,0:T(8,128)S(1)}, f32[72,72]{1,0:T(8,128)}, u32[]{:S(2)}) copy-start(f32[72,72]{1,0:T(8,128)} %param.27) | copy-start | bytes 62212
  170.1 33.9 %copy-start.5 = (bf16[1,2,2048,128]{3,2,1,0:T(8,128)(2,1)S(1)}, bf16[1,2,2048,128]{3,2,1,0:T(8,128)(2,1)}, u32[]{:S(2)}) copy-start(bf16[1,2,2048,128]{3,2,1,0:T(8,128)(2,1)} %param.29) | copy-start | bytes 3145732
  187.2 34.8 %all-to-all-start = ((s32[2,32,128]{2,0,1:T(2,128)}), s32[2,32,128]{2,0,1:T(2,128)S(1)}, u32[]{:S(2)}, u32[]{:S(2)}) async-start(s32[2,32,128]{2,0,1:T(2,128)} %fusion.79), calls=%async_computation | async-start | bytes 65536 | tf_op jit(solution)/shard_map/all_to_all | solution.py:138
  222.0 12.3 %copy-start.1 = (f32[1,72,8,128]{3,2,1,0:T(8,128)S(1)}, f32[1,72,8,128]{3,2,1,0:T(8,128)}, u32[]{:S(2)}) copy-start(f32[1,72,8,128]{3,2,1,0:T(8,128)} %param.24) | copy-start | bytes 884740
  222.0 110.8 %all-to-all-start.1 = ((bf16[2,32,128,128]{3,2,0,1:T(8,128)(2,1)}), bf16[2,32,128,128]{3,2,0,1:T(8,128)(2,1)S(1)}, u32[]{:S(2)}, u32[]{:S(2)}) async-start(bf16[2,32,128,128]{3,2,0,1:T(8,128)(2,1)} %maximum_select_fusion), calls=%async_computation.1 | async-start | bytes 4194304 | tf_op jit(solution)/shard_map/all_to_all | solution.py:149
  234.4 7.1 %collective-permute-start = (bf16[1,72,8,128]{3,1,2,0:T(8,128)(2,1)S(1)}, bf16[1,72,8,128]{3,1,2,0:T(8,128)(2,1)S(1)}, u32[]{:S(2)}, u32[]{:S(2)}) collective-permute-start(bf16[1,72,8,128]{3,1,2,0:T(8,128)(2,1)S(1)} %copy.80), channel_id=1, source_target_pairs={{32,0},{64,32},{96,64},{128,96},{160,128},{192,160},{224,192},{256... | collective-permute-start | bytes 442376 | tf_op jit(solution)/shard_map/ppermute | solution.py:25
  242.5 128.3 %collective-permute-start.1 = (f32[1,72,1,128]{3,1,2,0:T(8,128)}, f32[1,72,1,128]{3,1,2,0:T(8,128)S(1)}, u32[]{:S(2)}, u32[]{:S(2)}) collective-permute-start(f32[1,72,1,128]{3,1,2,0:T(8,128)} %get-tuple-element.342), channel_id=1, source_target_pairs={{1,0},{2,1},{3,2},{4,3},{5,4},{6,5},{7,6},{8,7},{9,8},{10,9},{11,1... | collective-permute-start | bytes 110600 | tf_op jit(solution)/shard_map/ppermute | solution.py:17
  243.5 127.2 %collective-permute-start.2 = (f32[1,72,1,128]{3,1,2,0:T(8,128)}, f32[1,72,1,128]{3,1,2,0:T(8,128)}, u32[]{:S(2)}, u32[]{:S(2)}) collective-permute-start(f32[1,72,1,128]{3,1,2,0:T(8,128)} %get-tuple-element.343), channel_id=1, source_target_pairs={{0,1},{1,2},{2,3},{3,4},{4,5},{5,6},{6,7},{7,8},{8,9},{9,10},{10,1... | collective-permute-start | bytes 110600 | tf_op jit(solution)/shard_map/ppermute | solution.py:16
  333.0 3.9 %copy-start.6 = (bf16[8,72,128]{2,1,0:T(8,128)(2,1)S(1)}, bf16[8,72,128]{2,1,0:T(8,128)(2,1)}, u32[]{:S(2)}) copy-start(bf16[8,72,128]{2,1,0:T(8,128)(2,1)} %param.28) | copy-start | bytes 442372
  343.9 2.3 copy-start.18
  343.9 2.3 copy-start.19
  343.9 2.3 copy-start.20
  343.9 2.3 copy-start.21
  343.9 2.3 copy-start.22
  346.2 1.0 copy-start.10
  346.3 1.0 copy-start.11
  346.3 1.0 copy-start.12
  348.9 18.4 %copy-start.13 = (pred[4096]{0:T(1024)(128)(4,1)S(1)}, pred[4096]{0:T(1024)(128)(4,1)}, u32[]{:S(2)}) copy-start(pred[4096]{0:T(1024)(128)(4,1)} %get-tuple-element.348) | copy-start | bytes 12292
  348.9 18.4 %copy-start.14 = (pred[4096]{0:T(1024)(128)(4,1)S(1)}, pred[4096]{0:T(1024)(128)(4,1)}, u32[]{:S(2)}) copy-start(pred[4096]{0:T(1024)(128)(4,1)} %get-tuple-element.349) | copy-start | bytes 12292
  348.9 18.4 %copy-start.15 = (pred[4096]{0:T(1024)(128)(4,1)S(1)}, pred[4096]{0:T(1024)(128)(4,1)}, u32[]{:S(2)}) copy-start(pred[4096]{0:T(1024)(128)(4,1)} %get-tuple-element.350) | copy-start | bytes 12292
  348.9 18.4 %copy-start.16 = (pred[4096]{0:T(1024)(128)(4,1)S(1)}, pred[4096]{0:T(1024)(128)(4,1)}, u32[]{:S(2)}) copy-start(pred[4096]{0:T(1024)(128)(4,1)} %get-tuple-element.351) | copy-start | bytes 12292
  348.9 18.4 %copy-start.17 = (pred[4096]{0:T(1024)(128)(4,1)S(1)}, pred[4096]{0:T(1024)(128)(4,1)}, u32[]{:S(2)}) copy-start(pred[4096]{0:T(1024)(128)(4,1)} %get-tuple-element.352) | copy-start | bytes 12292
  367.3 2.4 copy-start.9
  369.7 1.0 copy-start.8
  369.7 1.0 copy-start.3
  369.7 1.1 copy-start.4
  370.6 5.1 %copy-start.7 = (f32[72,1024]{1,0:T(8,128)S(1)}, f32[72,1024]{1,0:T(8,128)}, u32[]{:S(2)}) copy-start(f32[72,1024]{1,0:T(8,128)} %custom-call) | copy-start | bytes 884740
  372.4 8.6 %collective-permute-start.3 = (f32[1,72,1,128]{3,1,2,0:T(8,128)S(1)}, f32[1,72,1,128]{3,1,2,0:T(8,128)S(1)}, u32[]{:S(2)}, u32[]{:S(2)}) collective-permute-start(f32[1,72,1,128]{3,1,2,0:T(8,128)S(1)} %get-tuple-element.340), channel_id=1, source_target_pairs={{1,0},{2,1},{3,2},{4,3},{5,4},{6,5},{7,6},{8,7},{9,8},{10,9},{11,1... | collective-permute-start | bytes 110600 | tf_op jit(solution)/shard_map/ppermute | solution.py:17
  373.7 7.3 %collective-permute-start.4 = (f32[1,72,1,128]{3,1,2,0:T(8,128)S(1)}, f32[1,72,1,128]{3,1,2,0:T(8,128)S(1)}, u32[]{:S(2)}, u32[]{:S(2)}) collective-permute-start(f32[1,72,1,128]{3,1,2,0:T(8,128)S(1)} %get-tuple-element.341), channel_id=1, source_target_pairs={{0,1},{1,2},{2,3},{3,4},{4,5},{5,6},{6,7},{7,8},{8,9},{9,10},{10,1... | collective-permute-start | bytes 110600 | tf_op jit(solution)/shard_map/ppermute | solution.py:16
  375.7 5.3 %copy-start.2 = (f32[1,72,8,128]{3,2,1,0:T(8,128)S(1)}, f32[1,72,8,128]{3,2,1,0:T(8,128)}, u32[]{:S(2)}) copy-start(f32[1,72,8,128]{3,2,1,0:T(8,128)} %param.24) | copy-start | bytes 884740
where the time goes:
time: 385 us; the launch traced here: 382 us
  loops' own time  126 us (33%)
  waiting for transfers between devices  92.2 us (24%)
  matrix products  89.7 us (23%)
  starting transfers between devices  36.2 us (9%)
  local copies, waits for them, and re-layouts  29.5 us (8%)
  other arithmetic  7.94 us (2%)
    another operation x1, loops' own time, local(): row_ids = lax.map(tile_rows, starts.T).transpose(1, 0, 2)  125 us
    all_to_all x1, waiting for transfers between devices, local(): lax.all_to_all(picked, 'tile', split_axis=1, concat_axis=1, tiled=True)  88 us
    dot_general x32, matrix products, select_block(): jnp.dot(onehot, table, preferred_element_type=jnp.float32, precision=prec...  46.7 us
    dot_general x16, matrix products, add_block(): jnp.dot(block_vals, onehot, preferred_element_type=jnp.float32)  23.1 us
    slice x32, local copies, waits for them, and re-layouts, tile_rows(): tile_starts[moment]  18.7 us
    dot_general x16, matrix products, jacobian_rows(): lax.dot_general(jacobians[block], row_vals, (((1,), (1,)), ((), ())), pre...  18.1 us
    all_to_all x1, starting transfers between devices, local(): lax.all_to_all(meta_out, 'tile', split_axis=1, concat_axis=1, tiled=True)  16.7 us
    all_to_all x1, starting transfers between devices, local(): lax.all_to_all(picked, 'tile', split_axis=1, concat_axis=1, tiled=True)  12.3 us
  transfers between devices with their start and end apart: 7, of which 2 were waited for; matrix products, arithmetic and copies ran while one was open for 16% of the time, Pallas kernels for 0%

commit v1 on v0

v1 whole, which is shorter than its diff:
```python
import jax
import jax.numpy as jnp
from jax import lax
from jax.experimental import pallas as pl
from jax.experimental.pallas import tpu as pltpu
from jax.sharding import PartitionSpec as P

CAP = 128
LO = 256
META = 8
F32 = jnp.float32
BF16 = jnp.bfloat16
NT = (((1,), (1,)), ((), ()))
VMEM = pl.BlockSpec(memory_space=pltpu.VMEM)
SMEM = pl.BlockSpec(memory_space=pltpu.SMEM)
PARAMS = pltpu.CompilerParams(vmem_limit_bytes=48 * 2**20)


def pack_kernel(counts, deps, order, cells, blocks, jac, wire, listed):
    kinds, width, _ = jac.shape
    tiles = wire.shape[0]
    rows = deps.shape[2]
    parts = rows // LO
    high = width + META
    jac_all = jnp.concatenate([jac[b].astype(F32) for b in range(kinds)], axis=0).astype(BF16)
    meta_row = lax.broadcasted_iota(jnp.int32, (META, LO), 0)
    sub = lax.broadcasted_iota(jnp.int32, (LO, LO), 0)
    for m in range(2):
        pieces = []
        for j in range(parts):
            span = slice(j * LO, (j + 1) * LO)
            prod = lax.dot_general(jac_all, deps[0, m, span, :], NT, preferred_element_type=F32)
            kind = blocks[0, m : m + 1, span]
            vals = prod[:width]
            for b in range(1, kinds):
                vals = jnp.where(kind == b, prod[b * width : (b + 1) * width], vals)
            cell = cells[0, m : m + 1, span]
            meta = jnp.where(meta_row == 2 * m, cell >> 8, 0)
            meta = jnp.where(meta_row == 2 * m + 1, cell & (LO - 1), meta)
            pieces.append(jnp.concatenate([vals, meta.astype(F32)], axis=0).astype(BF16))
        stacked = jnp.concatenate(pieces, axis=0)
        for n in range(parts):
            want = order[0, m, :, n * LO : (n + 1) * LO]
            onehot = (sub == (want & (LO - 1))).astype(F32).astype(BF16)
            both = jnp.dot(stacked, onehot, preferred_element_type=F32)
            part = want >> 8
            got = both[:high]
            for h in range(1, parts):
                got = jnp.where(part == h, both[h * high : (h + 1) * high], got)
            listed[m, 2 * n] = got[:, :CAP]
            listed[m, 2 * n + 1] = got[:, CAP:]
        listed[m, 2 * parts] = jnp.zeros((high, CAP), F32)
        listed[m, 2 * parts + 1] = jnp.zeros((high, CAP), F32)

    lane = lax.broadcasted_iota(jnp.int32, (high, CAP), 1)
    meta_lane = lax.broadcasted_iota(jnp.int32, (META, CAP), 1)
    meta_sub = lax.broadcasted_iota(jnp.int32, (META, CAP), 0)

    def window(m, start):
        base = start >> 7
        shift = start & (CAP - 1)
        back = (CAP - shift) & (CAP - 1)
        near = pltpu.roll(listed[m, base], back, 1)
        far = pltpu.roll(listed[m, base + 1], back, 1)
        return jnp.where(lane < CAP - shift, near, far)

    def cut(q, starts):
        sizes = [counts[0, m, 0, q] for m in range(2)]
        got = [window(m, starts[m]) for m in range(2)]
        meta = [jnp.where(meta_lane < sizes[m], got[m][width:], -1.0) for m in range(2)]
        meta = jnp.where(meta_sub < 2, meta[0], meta[1])
        wire[q] = jnp.concatenate([got[0][:width], meta, got[1][:width]], axis=0).astype(BF16)
        return tuple(starts[m] + sizes[m] for m in range(2))

    lax.fori_loop(0, tiles, cut, (jnp.int32(0), jnp.int32(0)))


def scatter(wire, m, width):
    tiles = wire.shape[0]
    group = 4
    lanes = group * CAP
    low = lax.broadcasted_iota(jnp.int32, (LO, lanes), 0)
    first = 0 if m == 0 else width + META
    total = None
    for s in range(0, tiles, group):
        vals = [wire[s + i, first : first + width, :].astype(F32) for i in range(group)]
        meta = [wire[s + i, width - META : width + META, :].astype(F32) for i in range(group)]
        vals = jnp.concatenate(vals, axis=1)
        meta = jnp.concatenate(meta, axis=1).astype(jnp.int32)
        cell_hi = meta[META + 2 * m : META + 2 * m + 1]
        cell_lo = meta[META + 2 * m + 1 : META + 2 * m + 2]
        split = [jnp.where(cell_hi == h, vals, 0.0) for h in range(4)]
        left = jnp.concatenate(split, axis=0).astype(BF16)
        right = (low == cell_lo).astype(F32).astype(BF16)
        part = lax.dot_general(left, right, NT, preferred_element_type=F32)
        total = part if total is None else total + part
    return total


def mixed_kernel(wire, first_step, mix_t, mixed, west, east):
    width = mix_t.shape[0]
    total = scatter(wire, 1, width)
    mix = mix_t[...]
    mix_hi = mix.astype(BF16)
    mix_lo = (mix - mix_hi.astype(F32)).astype(BF16)
    for h in range(4):
        start = jnp.concatenate([first_step[2 * h], first_step[2 * h + 1]], axis=1)
        field = total[h * width : (h + 1) * width] - start
        field_hi = field.astype(BF16)
        field_lo = (field - field_hi.astype(F32)).astype(BF16)
        out = jnp.dot(mix_hi, field_hi, preferred_element_type=F32)
        out += jnp.dot(mix_hi, field_lo, preferred_element_type=F32)
        out += jnp.dot(mix_lo, field_hi, preferred_element_type=F32)
        mixed[2 * h] = out[:, :CAP]
        mixed[2 * h + 1] = out[:, CAP:]
        if h == 0:
            west[...] = out[:, :CAP]
        if h == 3:
            east[...] = out[:, CAP:]


def direct_kernel(wire, multiplier, base):
    width = multiplier.shape[1]
    total = scatter(wire, 0, width)
    for h in range(4):
        part = total[h * width : (h + 1) * width]
        base[2 * h] = multiplier[2 * h] + part[:, :CAP]
        base[2 * h + 1] = multiplier[2 * h + 1] + part[:, CAP:]


def final_kernel(mixed, west, east, diag, side, base, out):
    lons, width, lats = mixed.shape
    lane = lax.broadcasted_iota(jnp.int32, (width, lats), 1)
    rows = []
    for i in range(lons):
        here = mixed[i]
        beside = (mixed[i - 1] if i else west[...]) + (mixed[i + 1] if i + 1 < lons else east[...])
        north = jnp.where(lane == lats - 1, 0.0, pltpu.roll(here, lats - 1, 1))
        south = jnp.where(lane == 0, 0.0, pltpu.roll(here, 1, 1))
        rows.append(base[i] + diag[i] * here + side[i] * (beside + north + south))
    out[...] = jnp.stack(rows, axis=1)


def halo(first, last):
    count = lax.axis_size("tile")
    up = [(i, (i + 1) % count) for i in range(count)]
    down = [(j, i) for i, j in up]
    return lax.ppermute(last, "tile", up), lax.ppermute(first, "tile", down)


def local(
    multiplier,
    coef_diag,
    coef_side,
    mixing,
    jacobians,
    departures,
    counts,
    row_order,
    obs_cell,
    obs_block,
):
    tiles = lax.axis_size("tile")
    _, width, lons, lats = multiplier.shape
    rows = departures.shape[2]
    high = 2 * width + META
    wire = pl.pallas_call(
        pack_kernel,
        out_shape=jax.ShapeDtypeStruct((tiles, high, CAP), BF16),
        in_specs=[SMEM] + [VMEM] * 5,
        out_specs=VMEM,
        scratch_shapes=[pltpu.VMEM((2, rows // CAP + 2, width + META, CAP), F32)],
        compiler_params=PARAMS,
        name="pack",
    )(counts, departures, row_order, obs_cell, obs_block, jacobians)
    wire, multiplier, coef_diag, coef_side, mixing = lax.optimization_barrier(
        (wire, multiplier, coef_diag, coef_side, mixing)
    )
    received = lax.all_to_all(wire, "tile", split_axis=0, concat_axis=0, tiled=True)

    mult_t = multiplier[0].transpose(1, 0, 2)
    diag_t = coef_diag[0].transpose(1, 0, 2)
    side_t = coef_side[0].transpose(1, 0, 2)
    mix_t = mixing.T
    windows = lax.axis_size("win")
    following = lax.ppermute(
        mult_t.astype(BF16), "win", [(i, i - 1) for i in range(1, windows)]
    ).astype(F32)
    mixed = jnp.einsum("cd,xcy->xdy", mixing, following, precision=lax.Precision.HIGHEST)
    west, east = halo(mixed[0], mixed[-1])
    rimmed = jnp.concatenate([west[None], mixed, east[None]], axis=0)
    padded = jnp.pad(mixed, ((0, 0), (0, 0), (1, 1)))
    beside = rimmed[2:] + rimmed[:-2] + padded[:, :, 2:] + padded[:, :, :-2]
    first_step = diag_t * mixed + side_t * beside

    field = jax.ShapeDtypeStruct((lons, width, lats), F32)
    edge = jax.ShapeDtypeStruct((width, lats), F32)
    mixed, first, last = pl.pallas_call(
        mixed_kernel,
        out_shape=(field, edge, edge),
        in_specs=[VMEM] * 3,
        out_specs=(VMEM,) * 3,
        compiler_params=PARAMS,
        name="mix",
    )(received, first_step, mix_t)
    west, east = halo(first, last)
    base = pl.pallas_call(
        direct_kernel,
        out_shape=field,
        in_specs=[VMEM] * 2,
        out_specs=VMEM,
        compiler_params=PARAMS,
        name="direct",
    )(received, mult_t)
    out = pl.pallas_call(
        final_kernel,
        out_shape=jax.ShapeDtypeStruct((width, lons, lats), F32),
        in_specs=[VMEM] * 6,
        out_specs=VMEM,
        compiler_params=PARAMS,
        name="final",
    )(mixed, west, east, diag_t, side_t, base)
    return out[None]


def solution(mesh):
    in_specs = (
        P("win", None, "tile", None),
        P("win", None, "tile", None),
        P("win", None, "tile", None),
        P(),
        P(),
        P("win", None, "tile", None),
        P("win", None, "tile", None),
        P("win", None, "tile", None),
        P("win", None, "tile"),
        P("win", None, "tile"),
    )
    out_specs = P("win", None, "tile", None)
    return jax.shard_map(local, mesh=mesh, in_specs=in_specs, out_specs=out_specs, check_vma=False)
```

time: 385 us -> 101 us (0.26)
  loops' own time: 126 us -> 0 us
  matrix products: 89.7 us -> 0.33 us
  waiting for transfers between devices: 92.2 us -> 61.1 us
  local copies, waits for them, and re-layouts: 29.5 us -> 5.29 us
  starting transfers between devices: 36.2 us -> 21.5 us
  Pallas kernels: 0 us -> 10.9 us
  other arithmetic: 7.94 us -> 0.23 us
    another operation x7 -> x0, loops' own time: 126 us -> none  [the longest x1 125 us: local(): row_ids = lax.map(tile_rows, starts.T).transpose(1, 0, 2)]
    dot_general x66 -> x1, matrix products: 89.7 us -> 0.33 us  [local(): jnp.einsum('cd,xcy->xdy', mixing, following, precision=lax.Precision.HIGH...]
    all_to_all x2 -> x1, waiting for transfers between devices: 88 us -> 9.84 us  [local(): lax.all_to_all(wire, 'tile', split_axis=0, concat_axis=0, tiled=True)]
    ppermute x5, waiting for transfers between devices: 4.18 us -> 51.3 us  [the longest x4 45.5 us: halo(): return (lax.ppermute(last, 'tile', up), lax.ppermute(first, 'tile', down))]
    slice x69 -> x0, local copies, waits for them, and re-layouts: 20.2 us -> none  [the longest x32 18.7 us: tile_rows(): tile_starts[moment]]
    all_to_all x2 -> x1, starting transfers between devices: 29.1 us -> 16.9 us  [local(): lax.all_to_all(wire, 'tile', split_axis=0, concat_axis=0, tiled=True)]
    pallas_call x0 -> x4, Pallas kernels: none -> 10.9 us  [the longest x1 7.67 us: local(): pl.pallas_call(pack_kernel, out_shape=jax.ShapeDtypeStruct((tiles, high,...]
    dynamic_slice x112 -> x0, local copies, waits for them, and re-layouts: 5.36 us -> none  [the longest x32 2.64 us: tile_rows(): lax.dynamic_slice_in_dim(padded_order[moment], tile_starts[moment], capac...]
  transfers between devices with their start and end apart: 7 -> 6, of which waited for: 2 -> 5; matrix products, arithmetic and copies ran while one was open for 16% -> 1% of each run, Pallas kernels for 0% -> 1%
where the time goes in v1:
time: 101 us; the launch traced here: 99.5 us
  waiting for transfers between devices  61.1 us (60%)
  starting transfers between devices  21.5 us (21%)
  Pallas kernels  10.9 us (11%)
  local copies, waits for them, and re-layouts  5.29 us (5%)
    ppermute x4, waiting for transfers between devices, halo(): return (lax.ppermute(last, 'tile', up), lax.ppermute(first, 'tile', down))  45.5 us
    all_to_all x1, starting transfers between devices, local(): lax.all_to_all(wire, 'tile', split_axis=0, concat_axis=0, tiled=True)  16.9 us
    all_to_all x1, waiting for transfers between devices, local(): lax.all_to_all(wire, 'tile', split_axis=0, concat_axis=0, tiled=True)  9.84 us
    pallas_call x1, Pallas kernels, local(): pl.pallas_call(pack_kernel, out_shape=jax.ShapeDtypeStruct((tiles, high,...  7.67 us
    ppermute x1, waiting for transfers between devices, local(): lax.ppermute(mult_t.astype(BF16), 'win', [(i, i - 1) for i in range(1, wi...  5.81 us
    unnamed x20, local copies, waits for them, and re-layouts  4.98 us
    ppermute x4, starting transfers between devices, halo(): return (lax.ppermute(last, 'tile', up), lax.ppermute(first, 'tile', down))  3.31 us
  transfers between devices with their start and end apart: 6, of which 5 were waited for; matrix products, arithmetic and copies ran while one was open for 1% of the time, Pallas kernels for 1%

profile of v1, /device:TPU:1, one launch (start us, length us, event | category | flops | bytes accessed | tf_op | source)
XLA Modules:
  0.0 99.5 jit_solution(5967339304487809285)
XLA Ops:
  0.0 0.0 copy-start
  0.0 1.2 %copy-done = bf16[1,2,2048,128]{3,2,1,0:T(8,128)(2,1)S(1)} copy-done((bf16[1,2,2048,128]{3,2,1,0:T(8,128)(2,1)S(1)}, bf16[1,2,2048,128]{3,2,1,0:T(8,128)(2,1)}, u32[]{:S(2)}) %copy-start) | copy-done | bytes 1048600
  1.2 0.0 copy-start.1
  1.2 0.9 copy-done.1
  2.1 0.0 copy-start.2
  2.1 0.7 copy-done.2
  2.9 0.0 copy-start.3
  2.9 0.7 copy-done.3
  3.6 0.0 copy-start.4
  3.6 0.7 copy-done.4
  4.3 0.0 copy-start.5
  4.3 0.7 copy-done.5
  5.0 7.7 %pack.1 = bf16[32,152,128]{2,1,0:T(8,128)(2,1)} custom-call(s32[1,2,1,32]{3,2,1,0:T(1,128)S(1)} %copy-done.5, bf16[1,2,2048,128]{3,2,1,0:T(8,128)(2,1)S(1)} %copy-done, s32[1,2,1,2048]{3,2,1,0:T(1,128)S(1)} %copy-done.2, s32[1,2,2048]{2,1,0:T(2,128)S(1)} %copy-done.3, s32[1,2,2048]{2,1,0:T(2,128)S(1)} %copy-done.4, bf16[8,72,128]{2,1,0:T(8,128)(2,1)S(1)} %copy-done.1), custom_call_target="tpu_custom_call" | custom-call | tf_op jit(solution)/shard_map/pack/pallas_call | solution.py:167
  12.6 0.0 copy-start.8
  12.6 0.0 copy-start.9
  12.6 0.0 copy-start.6
  12.6 0.0 copy-start.7
  12.7 16.9 %all-to-all-start = ((bf16[32,152,128]{2,1,0:T(8,128)(2,1)}), bf16[32,152,128]{2,1,0:T(8,128)(2,1)S(1)}, u32[]{:S(2)}, u32[]{:S(2)}) async-start(bf16[32,152,128]{2,1,0:T(8,128)(2,1)} %pack.1), calls=%async_computation | async-start | bytes 2490368 | tf_op jit(solution)/shard_map/all_to_all | solution.py:179
  29.5 0.0 copy-done.8
  29.5 0.1 copy.28
  29.6 1.3 %collective-permute-start = (bf16[8,72,128]{2,1,0:T(8,128)(2,1)S(1)}, bf16[8,72,128]{2,1,0:T(8,128)(2,1)S(1)}, u32[]{:S(2)}, u32[]{:S(2)}) collective-permute-start(bf16[8,72,128]{2,1,0:T(8,128)(2,1)S(1)} %bitcast.36), channel_id=1, source_target_pairs={{32,0},{64,32},{96,64},{128,96},{160,128},{192,160},{224,192},{256... | collective-permute-start | bytes 442376 | tf_op jit(solution)/shard_map/ppermute | solution.py:186
  30.9 5.8 %collective-permute-done = bf16[8,72,128]{2,1,0:T(8,128)(2,1)S(1)} collective-permute-done((bf16[8,72,128]{2,1,0:T(8,128)(2,1)S(1)}, bf16[8,72,128]{2,1,0:T(8,128)(2,1)S(1)}, u32[]{:S(2)}, u32[]{:S(2)}) %collective-permute-start) | collective-permute-done | bytes 147488 | tf_op jit(solution)/shard_map/ppermute | solution.py:186
  36.7 0.0 copy-done.9
  36.7 0.3 convolution_bitcast_fusion
  37.1 2.3 %collective-permute-start.2 = (f32[72,128]{1,0:T(8,128)S(1)}, f32[72,128]{1,0:T(8,128)S(1)}, u32[]{:S(2)}, u32[]{:S(2)}) collective-permute-start(f32[72,128]{1,0:T(8,128)S(1)} %get-tuple-element.22), channel_id=1, source_target_pairs={{0,1},{1,2},{2,3},{3,4},{4,5},{5,6},{6,7},{7,8},{8,9},{9,10},{10,1... | collective-permute-start | bytes 110600 | tf_op jit(solution)/shard_map/ppermute | solution.py:148
  39.4 0.0 collective-permute-start.1
  39.4 0.1 copy.15
  39.5 38.6 %collective-permute-done.2 = f32[72,128]{1,0:T(8,128)S(1)} collective-permute-done((f32[72,128]{1,0:T(8,128)S(1)}, f32[72,128]{1,0:T(8,128)S(1)}, u32[]{:S(2)}, u32[]{:S(2)}) %collective-permute-start.2) | collective-permute-done | bytes 36896 | tf_op jit(solution)/shard_map/ppermute | solution.py:148
  78.1 5.4 %collective-permute-done.1 = f32[72,128]{1,0:T(8,128)S(1)} collective-permute-done((f32[72,128]{1,0:T(8,128)S(1)}, f32[72,128]{1,0:T(8,128)S(1)}, u32[]{:S(2)}, u32[]{:S(2)}) %collective-permute-start.1) | collective-permute-done | bytes 36896 | tf_op jit(solution)/shard_map/ppermute | solution.py:148
  83.5 0.0 copy-done.6
  83.5 0.0 copy-done.7
  83.5 0.2 fusion.3.first_step
  83.8 9.8 %all-to-all-done.wire = bf16[32,152,128]{2,1,0:T(8,128)(2,1)S(1)} async-done(((bf16[32,152,128]{2,1,0:T(8,128)(2,1)}), bf16[32,152,128]{2,1,0:T(8,128)(2,1)S(1)}, u32[]{:S(2)}, u32[]{:S(2)}) %all-to-all-start) | async-done | bytes 1245216 | tf_op jit(solution)/shard_map/all_to_all | solution.py:179
  93.6 1.3 %mix.1 = (f32[8,72,128]{2,1,0:T(8,128)S(1)}, f32[72,128]{1,0:T(8,128)S(1)}, f32[72,128]{1,0:T(8,128)S(1)}) custom-call(bf16[32,152,128]{2,1,0:T(8,128)(2,1)S(1)} %all-to-all-done.wire, f32[8,72,128]{2,1,0:T(8,128)S(1)} %fusion.3.first_step, f32[72,72]{1,0:T(8,128)S(1)} %bitcast.35), custom_call_target="tpu_custom_call" | custom-call | tf_op jit(solution)/shard_map/mix/pallas_call | solution.py:198
  94.9 0.0 collective-permute-start.3
  94.9 1.0 collective-permute-start.4
  95.9 0.1 copy_bitcast_fusion
  96.0 0.1 copy.27
  96.1 0.8 direct.1.base
  96.9 0.0 collective-permute-done.3.west
  96.9 1.4 %collective-permute-done.4.east = f32[72,128]{1,0:T(8,128)S(1)} collective-permute-done((f32[72,128]{1,0:T(8,128)S(1)}, f32[72,128]{1,0:T(8,128)S(1)}, u32[]{:S(2)}, u32[]{:S(2)}) %collective-permute-start.4) | collective-permute-done | bytes 36896 | tf_op jit(solution)/shard_map/ppermute | solution.py:148
  98.3 1.2 %final.1 = f32[72,8,128]{2,1,0:T(8,128)} custom-call(f32[8,72,128]{2,1,0:T(8,128)S(1)} %get-tuple-element.18.mixed, f32[72,128]{1,0:T(8,128)S(1)} %collective-permute-done.3.west, f32[72,128]{1,0:T(8,128)S(1)} %collective-permute-done.4.east, f32[8,72,128]{2,1,0:T(8,128)S(1)} %bitcast.34, f32[8,72,128]{2,1,0:T(8,128)S(1)} %get-tuple-element.23.side, ...), custom_call_target="tpu_custom_call" | custom-call | tf_op jit(solution)/shard_map/final/pallas_call | solution.py:215
  (1 shorter events, 0.0 us)
Async XLA Ops:
  0.0 1.2 %copy-start = (bf16[1,2,2048,128]{3,2,1,0:T(8,128)(2,1)S(1)}, bf16[1,2,2048,128]{3,2,1,0:T(8,128)(2,1)}, u32[]{:S(2)}) copy-start(bf16[1,2,2048,128]{3,2,1,0:T(8,128)(2,1)} %deps.1) | copy-start | bytes 3145732
  1.2 0.9 copy-start.1
  2.1 0.7 copy-start.2
  2.9 0.7 copy-start.3
  3.6 0.7 copy-start.4
  4.3 0.7 copy-start.5
  12.6 16.9 %copy-start.8 = (f32[1,72,8,128]{3,2,1,0:T(8,128)S(1)}, f32[1,72,8,128]{3,2,1,0:T(8,128)}, u32[]{:S(2)}) copy-start(f32[1,72,8,128]{3,2,1,0:T(8,128)} %param.10) | copy-start | bytes 884740
  12.6 24.1 %copy-start.9 = (f32[72,72]{1,0:T(8,128)S(1)}, f32[72,72]{1,0:T(8,128)}, u32[]{:S(2)}) copy-start(f32[72,72]{1,0:T(8,128)} %param.13) | copy-start | bytes 62212
  12.6 70.9 %copy-start.6 = (f32[1,72,8,128]{3,2,1,0:T(8,128)S(1)}, f32[1,72,8,128]{3,2,1,0:T(8,128)}, u32[]{:S(2)}) copy-start(f32[1,72,8,128]{3,2,1,0:T(8,128)} %param.11) | copy-start | bytes 884740
  12.6 70.9 %copy-start.7 = (f32[1,72,8,128]{3,2,1,0:T(8,128)S(1)}, f32[1,72,8,128]{3,2,1,0:T(8,128)}, u32[]{:S(2)}) copy-start(f32[1,72,8,128]{3,2,1,0:T(8,128)} %param.12) | copy-start | bytes 884740
  12.7 80.9 %all-to-all-start = ((bf16[32,152,128]{2,1,0:T(8,128)(2,1)}), bf16[32,152,128]{2,1,0:T(8,128)(2,1)S(1)}, u32[]{:S(2)}, u32[]{:S(2)}) async-start(bf16[32,152,128]{2,1,0:T(8,128)(2,1)} %pack.1), calls=%async_computation | async-start | bytes 2490368 | tf_op jit(solution)/shard_map/all_to_all | solution.py:179
  29.6 7.1 %collective-permute-start = (bf16[8,72,128]{2,1,0:T(8,128)(2,1)S(1)}, bf16[8,72,128]{2,1,0:T(8,128)(2,1)S(1)}, u32[]{:S(2)}, u32[]{:S(2)}) collective-permute-start(bf16[8,72,128]{2,1,0:T(8,128)(2,1)S(1)} %bitcast.36), channel_id=1, source_target_pairs={{32,0},{64,32},{96,64},{128,96},{160,128},{192,160},{224,192},{256... | collective-permute-start | bytes 442376 | tf_op jit(solution)/shard_map/ppermute | solution.py:186
  37.1 41.0 %collective-permute-start.2 = (f32[72,128]{1,0:T(8,128)S(1)}, f32[72,128]{1,0:T(8,128)S(1)}, u32[]{:S(2)}, u32[]{:S(2)}) collective-permute-start(f32[72,128]{1,0:T(8,128)S(1)} %get-tuple-element.22), channel_id=1, source_target_pairs={{0,1},{1,2},{2,3},{3,4},{4,5},{5,6},{6,7},{7,8},{8,9},{9,10},{10,1... | collective-permute-start | bytes 110600 | tf_op jit(solution)/shard_map/ppermute | solution.py:148
  39.4 44.1 %collective-permute-start.1 = (f32[72,128]{1,0:T(8,128)S(1)}, f32[72,128]{1,0:T(8,128)S(1)}, u32[]{:S(2)}, u32[]{:S(2)}) collective-permute-start(f32[72,128]{1,0:T(8,128)S(1)} %get-tuple-element.21), channel_id=1, source_target_pairs={{1,0},{2,1},{3,2},{4,3},{5,4},{6,5},{7,6},{8,7},{9,8},{10,9},{11,1... | collective-permute-start | bytes 110600 | tf_op jit(solution)/shard_map/ppermute | solution.py:148
  94.9 2.0 %collective-permute-start.3 = (f32[72,128]{1,0:T(8,128)S(1)}, f32[72,128]{1,0:T(8,128)S(1)}, u32[]{:S(2)}, u32[]{:S(2)}) collective-permute-start(f32[72,128]{1,0:T(8,128)S(1)} %get-tuple-element.19), channel_id=1, source_target_pairs={{0,1},{1,2},{2,3},{3,4},{4,5},{5,6},{6,7},{7,8},{8,9},{9,10},{10,1... | collective-permute-start | bytes 110600 | tf_op jit(solution)/shard_map/ppermute | solution.py:148
  94.9 3.4 %collective-permute-start.4 = (f32[72,128]{1,0:T(8,128)S(1)}, f32[72,128]{1,0:T(8,128)S(1)}, u32[]{:S(2)}, u32[]{:S(2)}) collective-permute-start(f32[72,128]{1,0:T(8,128)S(1)} %get-tuple-element.20), channel_id=1, source_target_pairs={{1,0},{2,1},{3,2},{4,3},{5,4},{6,5},{7,6},{8,7},{9,8},{10,9},{11,1... | collective-permute-start | bytes 110600 | tf_op jit(solution)/shard_map/ppermute | solution.py:148

commit v2 on v1

--- a/solution.py
+++ b/solution.py
@@ -12,33 +12,69 @@
 BF16 = jnp.bfloat16
 NT = (((1,), (1,)), ((), ()))
 VMEM = pl.BlockSpec(memory_space=pltpu.VMEM)
+HBM = pl.BlockSpec(memory_space=pltpu.HBM)
 SMEM = pl.BlockSpec(memory_space=pltpu.SMEM)
 PARAMS = pltpu.CompilerParams(vmem_limit_bytes=48 * 2**20)
-
-
-def pack_kernel(counts, deps, order, cells, blocks, jac, wire, listed):
+PACK_PARAMS = pltpu.CompilerParams(vmem_limit_bytes=60 * 2**20)
+
+
+def pack_kernel(
+    counts_hbm,
+    deps_hbm,
+    order_hbm,
+    cells_hbm,
+    blocks_hbm,
+    jac_hbm,
+    wire,
+    counts,
+    deps,
+    order,
+    cells,
+    blocks,
+    jac,
+    listed,
+    sems,
+):
+    loads = [
+        pltpu.make_async_copy(jac_hbm, jac, sems.at[0]),
+        pltpu.make_async_copy(blocks_hbm, blocks, sems.at[1]),
+        pltpu.make_async_copy(cells_hbm, cells, sems.at[2]),
+        pltpu.make_async_copy(deps_hbm.at[0, 0], deps.at[0], sems.at[3]),
+        pltpu.make_async_copy(order_hbm, order, sems.at[4]),
+        pltpu.make_async_copy(deps_hbm.at[0, 1], deps.at[1], sems.at[5]),
+        pltpu.make_async_copy(counts_hbm, counts, sems.at[6]),
+    ]
+    for load in loads:
+        load.start()
     kinds, width, _ = jac.shape
     tiles = wire.shape[0]
-    rows = deps.shape[2]
+    rows = deps.shape[1]
     parts = rows // LO
     high = width + META
-    jac_all = jnp.concatenate([jac[b].astype(F32) for b in range(kinds)], axis=0).astype(BF16)
     meta_row = lax.broadcasted_iota(jnp.int32, (META, LO), 0)
     sub = lax.broadcasted_iota(jnp.int32, (LO, LO), 0)
+    for load in loads[:4]:
+        load.wait()
+    jac_all = jnp.concatenate([jac[b].astype(F32) for b in range(kinds)], axis=0).astype(BF16)
     for m in range(2):
+        if m:
+            loads[5].wait()
         pieces = []
         for j in range(parts):
             span = slice(j * LO, (j + 1) * LO)
-            prod = lax.dot_general(jac_all, deps[0, m, span, :], NT, preferred_element_type=F32)
+            prod = lax.dot_general(jac_all, deps[m, span, :], NT, preferred_element_type=F32)
             kind = blocks[0, m : m + 1, span]
             vals = prod[:width]
             for b in range(1, kinds):
                 vals = jnp.where(kind == b, prod[b * width : (b + 1) * width], vals)
             cell = cells[0, m : m + 1, span]
-            meta = jnp.where(meta_row == 2 * m, cell >> 8, 0)
-            meta = jnp.where(meta_row == 2 * m + 1, cell & (LO - 1), meta)
-            pieces.append(jnp.concatenate([vals, meta.astype(F32)], axis=0).astype(BF16))
+            code = (CAP + (cell & (CAP - 1))) << ((cell >> 7) & 3)
+            code = jnp.where(cell >= 512, -code, code)
+            meta = jnp.where(meta_row == m, code, 0).astype(F32)
+            pieces.append(jnp.concatenate([vals, meta], axis=0).astype(BF16))
         stacked = jnp.concatenate(pieces, axis=0)
+        if m == 0:
+            loads[4].wait()
         for n in range(parts):
             want = order[0, m, :, n * LO : (n + 1) * LO]
             onehot = (sub == (want & (LO - 1))).astype(F32).astype(BF16)
@@ -51,7 +87,9 @@
             listed[m, 2 * n + 1] = got[:, CAP:]
         listed[m, 2 * parts] = jnp.zeros((high, CAP), F32)
         listed[m, 2 * parts + 1] = jnp.zeros((high, CAP), F32)
-
+    loads[6].wait()
+
+    slots = wire.reshape(tiles, 2 * width + 2, CAP)
     lane = lax.broadcasted_iota(jnp.int32, (high, CAP), 1)
     meta_lane = lax.broadcasted_iota(jnp.int32, (META, CAP), 1)
     meta_sub = lax.broadcasted_iota(jnp.int32, (META, CAP), 0)
@@ -64,31 +102,35 @@
         far = pltpu.roll(listed[m, base + 1], back, 1)
         return jnp.where(lane < CAP - shift, near, far)
 
-    def cut(q, starts):
+    starts = [jnp.int32(0), jnp.int32(0)]
+    for q in range(tiles):
         sizes = [counts[0, m, 0, q] for m in range(2)]
         got = [window(m, starts[m]) for m in range(2)]
-        meta = [jnp.where(meta_lane < sizes[m], got[m][width:], -1.0) for m in range(2)]
-        meta = jnp.where(meta_sub < 2, meta[0], meta[1])
-        wire[q] = jnp.concatenate([got[0][:width], meta, got[1][:width]], axis=0).astype(BF16)
-        return tuple(starts[m] + sizes[m] for m in range(2))
-
-    lax.fori_loop(0, tiles, cut, (jnp.int32(0), jnp.int32(0)))
+        meta = [jnp.where(meta_lane < sizes[m], got[m][width:], 0.0) for m in range(2)]
+        meta = jnp.where(meta_sub == 0, meta[0], meta[1])
+        block = jnp.concatenate([got[0][:width], got[1][:width], meta], axis=0)
+        slots[q] = block.astype(BF16)[: 2 * width + 2]
+        starts = [starts[m] + sizes[m] for m in range(2)]
 
 
 def scatter(wire, m, width):
     tiles = wire.shape[0]
+    slots = wire.reshape(tiles, 2 * width + 2, CAP)
     group = 4
     lanes = group * CAP
     low = lax.broadcasted_iota(jnp.int32, (LO, lanes), 0)
-    first = 0 if m == 0 else width + META
     total = None
     for s in range(0, tiles, group):
-        vals = [wire[s + i, first : first + width, :].astype(F32) for i in range(group)]
-        meta = [wire[s + i, width - META : width + META, :].astype(F32) for i in range(group)]
+        vals = [slots[s + i, m * width : (m + 1) * width, :].astype(F32) for i in range(group)]
+        meta = [slots[s + i, 2 * width : 2 * width + 2, :].astype(F32) for i in range(group)]
         vals = jnp.concatenate(vals, axis=1)
-        meta = jnp.concatenate(meta, axis=1).astype(jnp.int32)
-        cell_hi = meta[META + 2 * m : META + 2 * m + 1]
-        cell_lo = meta[META + 2 * m + 1 : META + 2 * m + 2]
+        code = jnp.concatenate(meta, axis=1)[m : m + 1].astype(jnp.int32)
+        size = jnp.abs(code)
+        scale = sum((size >= CAP << k).astype(jnp.int32) for k in range(1, 4))
+        cell = (size >> scale) - CAP + (scale << 7) + jnp.where(code < 0, 512, 0)
+        cell = jnp.where(code == 0, -1, cell)
+        cell_hi = cell >> 8
+        cell_lo = cell & (LO - 1)
         split = [jnp.where(cell_hi == h, vals, 0.0) for h in range(4)]
         left = jnp.concatenate(split, axis=0).astype(BF16)
         right = (low == cell_lo).astype(F32).astype(BF16)
@@ -119,25 +161,28 @@
             east[...] = out[:, CAP:]
 
 
-def direct_kernel(wire, multiplier, base):
-    width = multiplier.shape[1]
+def direct_kernel(wire, multiplier, mixed, diag, side, base):
+    lons, width, lats = multiplier.shape
     total = scatter(wire, 0, width)
-    for h in range(4):
-        part = total[h * width : (h + 1) * width]
-        base[2 * h] = multiplier[2 * h] + part[:, :CAP]
-        base[2 * h + 1] = multiplier[2 * h + 1] + part[:, CAP:]
-
-
-def final_kernel(mixed, west, east, diag, side, base, out):
-    lons, width, lats = mixed.shape
     lane = lax.broadcasted_iota(jnp.int32, (width, lats), 1)
-    rows = []
     for i in range(lons):
+        h, half = i // 2, (i % 2) * CAP
+        part = total[h * width : (h + 1) * width, half : half + CAP]
         here = mixed[i]
-        beside = (mixed[i - 1] if i else west[...]) + (mixed[i + 1] if i + 1 < lons else east[...])
-        north = jnp.where(lane == lats - 1, 0.0, pltpu.roll(here, lats - 1, 1))
-        south = jnp.where(lane == 0, 0.0, pltpu.roll(here, 1, 1))
-        rows.append(base[i] + diag[i] * here + side[i] * (beside + north + south))
+        beside = jnp.where(lane == lats - 1, 0.0, pltpu.roll(here, lats - 1, 1))
+        beside += jnp.where(lane == 0, 0.0, pltpu.roll(here, 1, 1))
+        if i:
+            beside += mixed[i - 1]
+        if i + 1 < lons:
+            beside += mixed[i + 1]
+        base[i] = multiplier[i] + part + diag[i] * here + side[i] * beside
+
+
+def final_kernel(base, west, east, side, out):
+    lons = base.shape[0]
+    rows = [base[i] for i in range(lons)]
+    rows[0] += side[0] * west[...]
+    rows[-1] += side[lons - 1] * east[...]
     out[...] = jnp.stack(rows, axis=1)
 
 
@@ -163,14 +208,22 @@
     tiles = lax.axis_size("tile")
     _, width, lons, lats = multiplier.shape
     rows = departures.shape[2]
-    high = 2 * width + META
     wire = pl.pallas_call(
         pack_kernel,
-        out_shape=jax.ShapeDtypeStruct((tiles, high, CAP), BF16),
-        in_specs=[SMEM] + [VMEM] * 5,
+        out_shape=jax.ShapeDtypeStruct((tiles, width + 1, 2, CAP), BF16),
+        in_specs=[HBM] * 6,
         out_specs=VMEM,
-        scratch_shapes=[pltpu.VMEM((2, rows // CAP + 2, width + META, CAP), F32)],
-        compiler_params=PARAMS,
+        scratch_shapes=[
+            pltpu.SMEM(counts.shape, jnp.int32),
+            pltpu.VMEM(departures.shape[1:], BF16),
+            pltpu.VMEM(row_order.shape, jnp.int32),
+            pltpu.VMEM(obs_cell.shape, jnp.int32),
+            pltpu.VMEM(obs_block.shape, jnp.int32),
+            pltpu.VMEM(jacobians.shape, BF16),
+            pltpu.VMEM((2, rows // CAP + 2, width + META, CAP), F32),
+            pltpu.SemaphoreType.DMA((7,)),
+        ],
+        compiler_params=PACK_PARAMS,
         name="pack",
     )(counts, departures, row_order, obs_cell, obs_block, jacobians)
     wire, multiplier, coef_diag, coef_side, mixing = lax.optimization_barrier(
@@ -207,19 +260,19 @@
     base = pl.pallas_call(
         direct_kernel,
         out_shape=field,
-        in_specs=[VMEM] * 2,
+        in_specs=[VMEM] * 5,
         out_specs=VMEM,
         compiler_params=PARAMS,
         name="direct",
-    )(received, mult_t)
+    )(received, mult_t, mixed, diag_t, side_t)
     out = pl.pallas_call(
         final_kernel,
         out_shape=jax.ShapeDtypeStruct((width, lons, lats), F32),
-        in_specs=[VMEM] * 6,
+        in_specs=[VMEM] * 4,
         out_specs=VMEM,
         compiler_params=PARAMS,
         name="final",
-    )(mixed, west, east, diag_t, side_t, base)
+    )(base, west, east, side_t)
     return out[None]
 
 

time: 101 us -> 92.4 us (0.915)
  local copies, waits for them, and re-layouts: 5.29 us -> 0.34 us
  waiting for transfers between devices: 61.1 us -> 58.6 us
    unnamed x20 -> x8, local copies, waits for them, and re-layouts: 4.98 us -> 0.03 us
    ppermute x4, waiting for transfers between devices: 45.5 us -> 43 us  [halo(): return (lax.ppermute(last, 'tile', up), lax.ppermute(first, 'tile', down))]
  transfers between devices with their start and end apart: 6 -> 6, of which waited for: 5 -> 4; matrix products, arithmetic and copies ran while one was open for 1% -> 1% of each run, Pallas kernels for 1% -> 1%
where the time goes in v2:
time: 92.4 us; the launch traced here: 91.6 us
  waiting for transfers between devices  58.6 us (63%)
  starting transfers between devices  21.5 us (23%)
  Pallas kernels  10.5 us (11%)
    ppermute x4, waiting for transfers between devices, halo(): return (lax.ppermute(last, 'tile', up), lax.ppermute(first, 'tile', down))  43 us
    all_to_all x1, starting transfers between devices, local(): lax.all_to_all(wire, 'tile', split_axis=0, concat_axis=0, tiled=True)  16.9 us
    all_to_all x1, waiting for transfers between devices, local(): lax.all_to_all(wire, 'tile', split_axis=0, concat_axis=0, tiled=True)  9.74 us
    pallas_call x1, Pallas kernels, local(): pl.pallas_call(pack_kernel, out_shape=jax.ShapeDtypeStruct((tiles, width...  6.57 us
    ppermute x1, waiting for transfers between devices, local(): lax.ppermute(mult_t.astype(BF16), 'win', [(i, i - 1) for i in range(1, wi...  5.81 us
    ppermute x4, starting transfers between devices, halo(): return (lax.ppermute(last, 'tile', up), lax.ppermute(first, 'tile', down))  3.33 us
  transfers between devices with their start and end apart: 6, of which 4 were waited for; matrix products, arithmetic and copies ran while one was open for 1% of the time, Pallas kernels for 1%

profile of v2, /device:TPU:1, one launch (start us, length us, event | category | flops | bytes accessed | tf_op | source)
XLA Modules:
  0.0 91.6 jit_solution(15657519717014495279)
XLA Ops:
  0.0 6.6 %pack.1 = bf16[32,73,2,128]{3,2,1,0:T(2,128)(2,1)} custom-call(s32[1,2,1,32]{3,2,1,0:T(1,128)} %counts_hbm.1, bf16[1,2,2048,128]{3,2,1,0:T(8,128)(2,1)} %deps_hbm.1, s32[1,2,1,2048]{3,2,1,0:T(1,128)} %order_hbm.1, s32[1,2,2048]{2,1,0:T(2,128)} %cells_hbm.1, s32[1,2,2048]{2,1,0:T(2,128)} %blocks_hbm.1, bf16[8,72,128]{2,1,0:T(8,128)(2,1)} %jac_hbm.1), custom_call_target="tpu_custom_call" | custom-call | tf_op jit(solution)/shard_map/pack/pallas_call | solution.py:211
  6.6 0.0 copy-start.2
  6.6 0.0 copy-start.3
  6.6 0.0 copy-start
  6.6 0.0 copy-start.1
  6.6 16.9 %all-to-all-start = ((bf16[32,73,2,128]{3,2,1,0:T(2,128)(2,1)}), bf16[32,73,2,128]{3,2,1,0:T(2,128)(2,1)S(1)}, u32[]{:S(2)}, u32[]{:S(2)}) async-start(bf16[32,73,2,128]{3,2,1,0:T(2,128)(2,1)} %pack.1), calls=%async_computation | async-start | bytes 2392064 | tf_op jit(solution)/shard_map/all_to_all | solution.py:232
  23.5 0.0 copy-done.2
  23.5 0.1 copy.28
  23.6 1.3 %collective-permute-start = (bf16[8,72,128]{2,1,0:T(8,128)(2,1)S(1)}, bf16[8,72,128]{2,1,0:T(8,128)(2,1)S(1)}, u32[]{:S(2)}, u32[]{:S(2)}) collective-permute-start(bf16[8,72,128]{2,1,0:T(8,128)(2,1)S(1)} %bitcast.36), channel_id=1, source_target_pairs={{32,0},{64,32},{96,64},{128,96},{160,128},{192,160},{224,192},{256... | collective-permute-start | bytes 442376 | tf_op jit(solution)/shard_map/ppermute | solution.py:239
  24.9 5.8 %collective-permute-done = bf16[8,72,128]{2,1,0:T(8,128)(2,1)S(1)} collective-permute-done((bf16[8,72,128]{2,1,0:T(8,128)(2,1)S(1)}, bf16[8,72,128]{2,1,0:T(8,128)(2,1)S(1)}, u32[]{:S(2)}, u32[]{:S(2)}) %collective-permute-start) | collective-permute-done | bytes 147488 | tf_op jit(solution)/shard_map/ppermute | solution.py:239
  30.7 0.0 copy-done.3
  30.7 0.3 convolution_bitcast_fusion
  31.1 1.1 %collective-permute-start.1 = (f32[72,128]{1,0:T(8,128)S(1)}, f32[72,128]{1,0:T(8,128)S(1)}, u32[]{:S(2)}, u32[]{:S(2)}) collective-permute-start(f32[72,128]{1,0:T(8,128)S(1)} %get-tuple-element.21), channel_id=1, source_target_pairs={{1,0},{2,1},{3,2},{4,3},{5,4},{6,5},{7,6},{8,7},{9,8},{10,9},{11,1... | collective-permute-start | bytes 110600 | tf_op jit(solution)/shard_map/ppermute | solution.py:193
  32.1 1.3 %collective-permute-start.2 = (f32[72,128]{1,0:T(8,128)S(1)}, f32[72,128]{1,0:T(8,128)S(1)}, u32[]{:S(2)}, u32[]{:S(2)}) collective-permute-start(f32[72,128]{1,0:T(8,128)S(1)} %get-tuple-element.22), channel_id=1, source_target_pairs={{0,1},{1,2},{2,3},{3,4},{4,5},{5,6},{6,7},{7,8},{8,9},{9,10},{10,1... | collective-permute-start | bytes 110600 | tf_op jit(solution)/shard_map/ppermute | solution.py:193
  33.4 0.1 copy.15
  33.5 42.0 %collective-permute-done.1 = f32[72,128]{1,0:T(8,128)S(1)} collective-permute-done((f32[72,128]{1,0:T(8,128)S(1)}, f32[72,128]{1,0:T(8,128)S(1)}, u32[]{:S(2)}, u32[]{:S(2)}) %collective-permute-start.1) | collective-permute-done | bytes 36896 | tf_op jit(solution)/shard_map/ppermute | solution.py:193
  75.5 0.0 collective-permute-done.2
  75.5 0.0 copy-done
  75.5 0.0 copy-done.1
  75.5 0.2 fusion.3.first_step
  75.8 9.7 %all-to-all-done.wire = bf16[32,73,2,128]{3,2,1,0:T(2,128)(2,1)S(1)} async-done(((bf16[32,73,2,128]{3,2,1,0:T(2,128)(2,1)}), bf16[32,73,2,128]{3,2,1,0:T(2,128)(2,1)S(1)}, u32[]{:S(2)}, u32[]{:S(2)}) %all-to-all-start) | async-done | bytes 1196064 | tf_op jit(solution)/shard_map/all_to_all | solution.py:232
  85.5 1.7 %mix.1 = (f32[8,72,128]{2,1,0:T(8,128)S(1)}, f32[72,128]{1,0:T(8,128)S(1)}, f32[72,128]{1,0:T(8,128)S(1)}) custom-call(bf16[32,73,2,128]{3,2,1,0:T(2,128)(2,1)S(1)} %all-to-all-done.wire, f32[8,72,128]{2,1,0:T(8,128)S(1)} %fusion.3.first_step, f32[72,72]{1,0:T(8,128)S(1)} %bitcast.35), custom_call_target="tpu_custom_call" | custom-call | tf_op jit(solution)/shard_map/mix/pallas_call | solution.py:251
  87.2 0.0 collective-permute-start.3
  87.2 1.0 %collective-permute-start.4 = (f32[72,128]{1,0:T(8,128)S(1)}, f32[72,128]{1,0:T(8,128)S(1)}, u32[]{:S(2)}, u32[]{:S(2)}) collective-permute-start(f32[72,128]{1,0:T(8,128)S(1)} %get-tuple-element.20), channel_id=1, source_target_pairs={{1,0},{2,1},{3,2},{4,3},{5,4},{6,5},{7,6},{8,7},{9,8},{10,9},{11,1... | collective-permute-start | bytes 110600 | tf_op jit(solution)/shard_map/ppermute | solution.py:193
  88.2 0.1 copy_bitcast_fusion
  88.3 0.1 copy.27
  88.3 1.3 %direct.1.base = f32[8,72,128]{2,1,0:T(8,128)S(1)} custom-call(bf16[32,73,2,128]{3,2,1,0:T(2,128)(2,1)S(1)} %all-to-all-done.wire, f32[8,72,128]{2,1,0:T(8,128)S(1)} %bitcast.34, f32[8,72,128]{2,1,0:T(8,128)S(1)} %get-tuple-element.18.mixed, f32[8,72,128]{2,1,0:T(8,128)S(1)} %get-tuple-element.24.diag, f32[8,72,128]{2,1,0:T(8,128)S(1)} %get-tuple-element.23.side), custom_call_target="tpu_custom_call" | custom-call | tf_op jit(solution)/shard_map/direct/pallas_call | solution.py:260
  89.6 0.0 collective-permute-done.3.west
  89.6 1.0 %collective-permute-done.4.east = f32[72,128]{1,0:T(8,128)S(1)} collective-permute-done((f32[72,128]{1,0:T(8,128)S(1)}, f32[72,128]{1,0:T(8,128)S(1)}, u32[]{:S(2)}, u32[]{:S(2)}) %collective-permute-start.4) | collective-permute-done | bytes 36896 | tf_op jit(solution)/shard_map/ppermute | solution.py:193
  90.6 1.0 %final.1 = f32[72,8,128]{2,1,0:T(8,128)} custom-call(f32[8,72,128]{2,1,0:T(8,128)S(1)} %direct.1.base, f32[72,128]{1,0:T(8,128)S(1)} %collective-permute-done.3.west, f32[72,128]{1,0:T(8,128)S(1)} %collective-permute-done.4.east, f32[8,72,128]{2,1,0:T(8,128)S(1)} %get-tuple-element.23.side), custom_call_target="tpu_custom_call" | custom-call | tf_op jit(solution)/shard_map/final/pallas_call | solution.py:268
  (1 shorter events, 0.0 us)
Async XLA Ops:
  6.6 17.0 %copy-start.2 = (f32[1,72,8,128]{3,2,1,0:T(8,128)S(1)}, f32[1,72,8,128]{3,2,1,0:T(8,128)}, u32[]{:S(2)}) copy-start(f32[1,72,8,128]{3,2,1,0:T(8,128)} %param.10) | copy-start | bytes 884740
  6.6 24.1 %copy-start.3 = (f32[72,72]{1,0:T(8,128)S(1)}, f32[72,72]{1,0:T(8,128)}, u32[]{:S(2)}) copy-start(f32[72,72]{1,0:T(8,128)} %param.13) | copy-start | bytes 62212
  6.6 68.9 %copy-start = (f32[1,72,8,128]{3,2,1,0:T(8,128)S(1)}, f32[1,72,8,128]{3,2,1,0:T(8,128)}, u32[]{:S(2)}) copy-start(f32[1,72,8,128]{3,2,1,0:T(8,128)} %param.11) | copy-start | bytes 884740
  6.6 68.9 %copy-start.1 = (f32[1,72,8,128]{3,2,1,0:T(8,128)S(1)}, f32[1,72,8,128]{3,2,1,0:T(8,128)}, u32[]{:S(2)}) copy-start(f32[1,72,8,128]{3,2,1,0:T(8,128)} %param.12) | copy-start | bytes 884740
  6.6 78.9 %all-to-all-start = ((bf16[32,73,2,128]{3,2,1,0:T(2,128)(2,1)}), bf16[32,73,2,128]{3,2,1,0:T(2,128)(2,1)S(1)}, u32[]{:S(2)}, u32[]{:S(2)}) async-start(bf16[32,73,2,128]{3,2,1,0:T(2,128)(2,1)} %pack.1), calls=%async_computation | async-start | bytes 2392064 | tf_op jit(solution)/shard_map/all_to_all | solution.py:232
  23.6 7.1 %collective-permute-start = (bf16[8,72,128]{2,1,0:T(8,128)(2,1)S(1)}, bf16[8,72,128]{2,1,0:T(8,128)(2,1)S(1)}, u32[]{:S(2)}, u32[]{:S(2)}) collective-permute-start(bf16[8,72,128]{2,1,0:T(8,128)(2,1)S(1)} %bitcast.36), channel_id=1, source_target_pairs={{32,0},{64,32},{96,64},{128,96},{160,128},{192,160},{224,192},{256... | collective-permute-start | bytes 442376 | tf_op jit(solution)/shard_map/ppermute | solution.py:239
  31.1 44.5 %collective-permute-start.1 = (f32[72,128]{1,0:T(8,128)S(1)}, f32[72,128]{1,0:T(8,128)S(1)}, u32[]{:S(2)}, u32[]{:S(2)}) collective-permute-start(f32[72,128]{1,0:T(8,128)S(1)} %get-tuple-element.21), channel_id=1, source_target_pairs={{1,0},{2,1},{3,2},{4,3},{5,4},{6,5},{7,6},{8,7},{9,8},{10,9},{11,1... | collective-permute-start | bytes 110600 | tf_op jit(solution)/shard_map/ppermute | solution.py:193
  32.1 43.4 %collective-permute-start.2 = (f32[72,128]{1,0:T(8,128)S(1)}, f32[72,128]{1,0:T(8,128)S(1)}, u32[]{:S(2)}, u32[]{:S(2)}) collective-permute-start(f32[72,128]{1,0:T(8,128)S(1)} %get-tuple-element.22), channel_id=1, source_target_pairs={{0,1},{1,2},{2,3},{3,4},{4,5},{5,6},{6,7},{7,8},{8,9},{9,10},{10,1... | collective-permute-start | bytes 110600 | tf_op jit(solution)/shard_map/ppermute | solution.py:193
  87.2 2.4 %collective-permute-start.3 = (f32[72,128]{1,0:T(8,128)S(1)}, f32[72,128]{1,0:T(8,128)S(1)}, u32[]{:S(2)}, u32[]{:S(2)}) collective-permute-start(f32[72,128]{1,0:T(8,128)S(1)} %get-tuple-element.19), channel_id=1, source_target_pairs={{0,1},{1,2},{2,3},{3,4},{4,5},{5,6},{6,7},{7,8},{8,9},{9,10},{10,1... | collective-permute-start | bytes 110600 | tf_op jit(solution)/shard_map/ppermute | solution.py:193
  87.2 3.4 %collective-permute-start.4 = (f32[72,128]{1,0:T(8,128)S(1)}, f32[72,128]{1,0:T(8,128)S(1)}, u32[]{:S(2)}, u32[]{:S(2)}) collective-permute-start(f32[72,128]{1,0:T(8,128)S(1)} %get-tuple-element.20), channel_id=1, source_target_pairs={{1,0},{2,1},{3,2},{4,3},{5,4},{6,5},{7,6},{8,7},{9,8},{10,9},{11,1... | collective-permute-start | bytes 110600 | tf_op jit(solution)/shard_map/ppermute | solution.py:193

commit v3 on v2

--- a/solution.py
+++ b/solution.py
@@ -8,6 +8,7 @@
 CAP = 128
 LO = 256
 META = 8
+OUT = 8
 F32 = jnp.float32
 BF16 = jnp.bfloat16
 NT = (((1,), (1,)), ((), ()))
@@ -25,14 +26,17 @@
     cells_hbm,
     blocks_hbm,
     jac_hbm,
-    wire,
+    wire_hbm,
     counts,
     deps,
     order,
     cells,
     blocks,
     jac,
-    listed,
+    listed0,
+    listed1,
+    codes,
+    wire,
     sems,
 ):
     loads = [
@@ -47,25 +51,36 @@
     for load in loads:
         load.start()
     kinds, width, _ = jac.shape
-    tiles = wire.shape[0]
+    tiles = wire_hbm.shape[0]
     rows = deps.shape[1]
     parts = rows // LO
     high = width + META
+    slots = wire.reshape(tiles, 2 * width + 2, CAP)
     meta_row = lax.broadcasted_iota(jnp.int32, (META, LO), 0)
-    sub = lax.broadcasted_iota(jnp.int32, (LO, LO), 0)
+    sub = lax.broadcasted_iota(jnp.int32, (LO, LO), 0).astype(F32).astype(BF16)
+    one, zero = jnp.ones((), BF16), jnp.zeros((), BF16)
+    lane = lax.broadcasted_iota(jnp.int32, (high, CAP), 1)
+    lane_row = lax.broadcasted_iota(jnp.int32, (2, CAP), 1)
     for load in loads[:4]:
         load.wait()
-    jac_all = jnp.concatenate([jac[b].astype(F32) for b in range(kinds)], axis=0).astype(BF16)
-    for m in range(2):
-        if m:
-            loads[5].wait()
+    half = kinds // 2
+    jac_pair = [jnp.concatenate([jac[b], jac[b + half]], axis=1).astype(F32) for b in range(half)]
+    jac_pair = jnp.concatenate(jac_pair, axis=0).astype(BF16)
+
+    def in_list_order(m, listed):
         pieces = []
         for j in range(parts):
             span = slice(j * LO, (j + 1) * LO)
-            prod = lax.dot_general(jac_all, deps[m, span, :], NT, preferred_element_type=F32)
             kind = blocks[0, m : m + 1, span]
+            dep = deps[m, span, :].T
+            low_kind = jnp.where(kind < half, 1.0, 0.0)
+            dep = jnp.concatenate(
+                [dep * low_kind.astype(BF16), dep * (1.0 - low_kind).astype(BF16)], axis=0
+            )
+            prod = jnp.dot(jac_pair, dep, preferred_element_type=F32)
+            kind = kind & (half - 1)
             vals = prod[:width]
-            for b in range(1, kinds):
+            for b in range(1, half):
                 vals = jnp.where(kind == b, prod[b * width : (b + 1) * width], vals)
             cell = cells[0, m : m + 1, span]
             code = (CAP + (cell & (CAP - 1))) << ((cell >> 7) & 3)
@@ -77,40 +92,54 @@
             loads[4].wait()
         for n in range(parts):
             want = order[0, m, :, n * LO : (n + 1) * LO]
-            onehot = (sub == (want & (LO - 1))).astype(F32).astype(BF16)
+            onehot = jnp.where(sub == (want & (LO - 1)).astype(F32).astype(BF16), one, zero)
             both = jnp.dot(stacked, onehot, preferred_element_type=F32)
             part = want >> 8
             got = both[:high]
             for h in range(1, parts):
                 got = jnp.where(part == h, both[h * high : (h + 1) * high], got)
-            listed[m, 2 * n] = got[:, :CAP]
-            listed[m, 2 * n + 1] = got[:, CAP:]
-        listed[m, 2 * parts] = jnp.zeros((high, CAP), F32)
-        listed[m, 2 * parts + 1] = jnp.zeros((high, CAP), F32)
-    loads[6].wait()
-
-    slots = wire.reshape(tiles, 2 * width + 2, CAP)
-    lane = lax.broadcasted_iota(jnp.int32, (high, CAP), 1)
-    meta_lane = lax.broadcasted_iota(jnp.int32, (META, CAP), 1)
-    meta_sub = lax.broadcasted_iota(jnp.int32, (META, CAP), 0)
-
-    def window(m, start):
+            listed[2 * n] = got[:, :CAP].astype(BF16)
+            listed[2 * n + 1] = got[:, CAP:].astype(BF16)
+        listed[2 * parts] = jnp.zeros((high, CAP), BF16)
+        listed[2 * parts + 1] = jnp.zeros((high, CAP), BF16)
+
+    def window(listed, start):
         base = start >> 7
         shift = start & (CAP - 1)
         back = (CAP - shift) & (CAP - 1)
-        near = pltpu.roll(listed[m, base], back, 1)
-        far = pltpu.roll(listed[m, base + 1], back, 1)
+        near = pltpu.roll(listed[base], back, 1)
+        far = pltpu.roll(listed[base + 1], back, 1)
         return jnp.where(lane < CAP - shift, near, far)
 
-    starts = [jnp.int32(0), jnp.int32(0)]
+    in_list_order(0, listed0)
+    loads[6].wait()
+    start = jnp.int32(0)
     for q in range(tiles):
-        sizes = [counts[0, m, 0, q] for m in range(2)]
-        got = [window(m, starts[m]) for m in range(2)]
-        meta = [jnp.where(meta_lane < sizes[m], got[m][width:], 0.0) for m in range(2)]
-        meta = jnp.where(meta_sub == 0, meta[0], meta[1])
-        block = jnp.concatenate([got[0][:width], got[1][:width], meta], axis=0)
-        slots[q] = block.astype(BF16)[: 2 * width + 2]
-        starts = [starts[m] + sizes[m] for m in range(2)]
+        size = counts[0, 0, 0, q]
+        got = window(listed0, start)
+        slots[q, :width] = got[:width]
+        code = got[width : width + 2]
+        codes[q] = jnp.where(lane_row < size, code.astype(F32), 0.0)
+        start += size
+    loads[5].wait()
+    in_list_order(1, listed1)
+    start = jnp.int32(0)
+    stores = []
+    for q in range(tiles):
+        size = counts[0, 1, 0, q]
+        got = window(listed1, start)
+        slots[q, width : 2 * width] = got[:width]
+        code = jnp.where(lane_row < size, got[width : width + 2].astype(F32), 0.0)
+        slots[q, 2 * width :] = (codes[q] + code).astype(BF16)
+        start += size
+        if (q + 1) % OUT == 0:
+            k = q // OUT
+            span = pl.ds(k * OUT, OUT)
+            store = pltpu.make_async_copy(wire.at[span], wire_hbm.at[span], sems.at[7 + k])
+            store.start()
+            stores.append(store)
+    for store in stores:
+        store.wait()
 
 
 def scatter(wire, m, width):
@@ -118,10 +147,13 @@
     slots = wire.reshape(tiles, 2 * width + 2, CAP)
     group = 4
     lanes = group * CAP
-    low = lax.broadcasted_iota(jnp.int32, (LO, lanes), 0)
+    high = width + META
+    first = m * (width - META)
+    low = lax.broadcasted_iota(jnp.int32, (LO, lanes), 0).astype(F32).astype(BF16)
+    one, zero = jnp.ones((), BF16), jnp.zeros((), BF16)
     total = None
     for s in range(0, tiles, group):
-        vals = [slots[s + i, m * width : (m + 1) * width, :].astype(F32) for i in range(group)]
+        vals = [slots[s + i, first : first + high, :] for i in range(group)]
         meta = [slots[s + i, 2 * width : 2 * width + 2, :].astype(F32) for i in range(group)]
         vals = jnp.concatenate(vals, axis=1)
         code = jnp.concatenate(meta, axis=1)[m : m + 1].astype(jnp.int32)
@@ -130,13 +162,14 @@
         cell = (size >> scale) - CAP + (scale << 7) + jnp.where(code < 0, 512, 0)
         cell = jnp.where(code == 0, -1, cell)
         cell_hi = cell >> 8
-        cell_lo = cell & (LO - 1)
-        split = [jnp.where(cell_hi == h, vals, 0.0) for h in range(4)]
-        left = jnp.concatenate(split, axis=0).astype(BF16)
-        right = (low == cell_lo).astype(F32).astype(BF16)
+        cell_lo = (cell & (LO - 1)).astype(F32).astype(BF16)
+        split = [vals * (cell_hi == h).astype(F32).astype(BF16) for h in range(4)]
+        left = jnp.concatenate(split, axis=0)
+        right = jnp.where(low == cell_lo, one, zero)
         part = lax.dot_general(left, right, NT, preferred_element_type=F32)
         total = part if total is None else total + part
-    return total
+    skip = m * META
+    return [total[h * high + skip : h * high + skip + width] for h in range(4)]
 
 
 def mixed_kernel(wire, first_step, mix_t, mixed, west, east):
@@ -147,7 +180,7 @@
     mix_lo = (mix - mix_hi.astype(F32)).astype(BF16)
     for h in range(4):
         start = jnp.concatenate([first_step[2 * h], first_step[2 * h + 1]], axis=1)
-        field = total[h * width : (h + 1) * width] - start
+        field = total[h] - start
         field_hi = field.astype(BF16)
         field_lo = (field - field_hi.astype(F32)).astype(BF16)
         out = jnp.dot(mix_hi, field_hi, preferred_element_type=F32)
@@ -167,7 +200,7 @@
     lane = lax.broadcasted_iota(jnp.int32, (width, lats), 1)
     for i in range(lons):
         h, half = i // 2, (i % 2) * CAP
-        part = total[h * width : (h + 1) * width, half : half + CAP]
+        part = total[h][:, half : half + CAP]
         here = mixed[i]
         beside = jnp.where(lane == lats - 1, 0.0, pltpu.roll(here, lats - 1, 1))
         beside += jnp.where(lane == 0, 0.0, pltpu.roll(here, 1, 1))
@@ -212,7 +245,7 @@
         pack_kernel,
         out_shape=jax.ShapeDtypeStruct((tiles, width + 1, 2, CAP), BF16),
         in_specs=[HBM] * 6,
-        out_specs=VMEM,
+        out_specs=HBM,
         scratch_shapes=[
             pltpu.SMEM(counts.shape, jnp.int32),
             pltpu.VMEM(departures.shape[1:], BF16),
@@ -220,8 +253,11 @@
             pltpu.VMEM(obs_cell.shape, jnp.int32),
             pltpu.VMEM(obs_block.shape, jnp.int32),
             pltpu.VMEM(jacobians.shape, BF16),
-            pltpu.VMEM((2, rows // CAP + 2, width + META, CAP), F32),
-            pltpu.SemaphoreType.DMA((7,)),
+            pltpu.VMEM((rows // CAP + 2, width + META, CAP), BF16),
+            pltpu.VMEM((rows // CAP + 2, width + META, CAP), BF16),
+            pltpu.VMEM((tiles, 2, CAP), F32),
+            pltpu.VMEM((tiles, width + 1, 2, CAP), BF16),
+            pltpu.SemaphoreType.DMA((7 + tiles // OUT,)),
         ],
         compiler_params=PACK_PARAMS,
         name="pack",

time: 92.4 us -> 91.2 us (0.987)
  Pallas kernels: 10.5 us -> 8.99 us
    pallas_call x1, Pallas kernels: 6.57 us -> 5.58 us  [local(): pl.pallas_call(pack_kernel, out_shape=jax.ShapeDtypeStruct((tiles, width...]
where the time goes in v3:
time: 91.2 us; the launch traced here: 90.4 us
  waiting for transfers between devices  58.8 us (64%)
  starting transfers between devices  21.5 us (24%)
  Pallas kernels  8.99 us (10%)
    ppermute x4, waiting for transfers between devices, halo(): return (lax.ppermute(last, 'tile', up), lax.ppermute(first, 'tile', down))  43.3 us
    all_to_all x1, starting transfers between devices, local(): lax.all_to_all(wire, 'tile', split_axis=0, concat_axis=0, tiled=True)  16.9 us
    all_to_all x1, waiting for transfers between devices, local(): lax.all_to_all(wire, 'tile', split_axis=0, concat_axis=0, tiled=True)  9.74 us
    ppermute x1, waiting for transfers between devices, local(): lax.ppermute(mult_t.astype(BF16), 'win', [(i, i - 1) for i in range(1, wi...  5.81 us
    pallas_call x1, Pallas kernels, local(): pl.pallas_call(pack_kernel, out_shape=jax.ShapeDtypeStruct((tiles, width...  5.58 us
    ppermute x4, starting transfers between devices, halo(): return (lax.ppermute(last, 'tile', up), lax.ppermute(first, 'tile', down))  3.33 us
  transfers between devices with their start and end apart: 6, of which 4 were waited for; matrix products, arithmetic and copies ran while one was open for 1% of the time, Pallas kernels for 1%

profile of v3, /device:TPU:1, one launch (start us, length us, event | category | flops | bytes accessed | tf_op | source)
XLA Modules:
  0.0 90.4 jit_solution(17742456311501547029)
XLA Ops:
  0.0 5.6 %pack.1 = bf16[32,73,2,128]{3,2,1,0:T(2,128)(2,1)} custom-call(s32[1,2,1,32]{3,2,1,0:T(1,128)} %counts_hbm.1, bf16[1,2,2048,128]{3,2,1,0:T(8,128)(2,1)} %deps_hbm.1, s32[1,2,1,2048]{3,2,1,0:T(1,128)} %order_hbm.1, s32[1,2,2048]{2,1,0:T(2,128)} %cells_hbm.1, s32[1,2,2048]{2,1,0:T(2,128)} %blocks_hbm.1, bf16[8,72,128]{2,1,0:T(8,128)(2,1)} %jac_hbm.1), custom_call_target="tpu_custom_call" | custom-call | tf_op jit(solution)/shard_map/pack/pallas_call | solution.py:244
  5.6 0.0 copy-start.2
  5.6 0.0 copy-start.3
  5.6 0.0 copy-start
  5.6 0.0 copy-start.1
  5.6 16.9 %all-to-all-start = ((bf16[32,73,2,128]{3,2,1,0:T(2,128)(2,1)}), bf16[32,73,2,128]{3,2,1,0:T(2,128)(2,1)S(1)}, u32[]{:S(2)}, u32[]{:S(2)}) async-start(bf16[32,73,2,128]{3,2,1,0:T(2,128)(2,1)} %pack.1), calls=%async_computation | async-start | bytes 2392064 | tf_op jit(solution)/shard_map/all_to_all | solution.py:268
  22.5 0.0 copy-done.2
  22.5 0.1 copy.28
  22.6 1.3 %collective-permute-start = (bf16[8,72,128]{2,1,0:T(8,128)(2,1)S(1)}, bf16[8,72,128]{2,1,0:T(8,128)(2,1)S(1)}, u32[]{:S(2)}, u32[]{:S(2)}) collective-permute-start(bf16[8,72,128]{2,1,0:T(8,128)(2,1)S(1)} %bitcast.36), channel_id=1, source_target_pairs={{32,0},{64,32},{96,64},{128,96},{160,128},{192,160},{224,192},{256... | collective-permute-start | bytes 442376 | tf_op jit(solution)/shard_map/ppermute | solution.py:275
  23.9 5.8 %collective-permute-done = bf16[8,72,128]{2,1,0:T(8,128)(2,1)S(1)} collective-permute-done((bf16[8,72,128]{2,1,0:T(8,128)(2,1)S(1)}, bf16[8,72,128]{2,1,0:T(8,128)(2,1)S(1)}, u32[]{:S(2)}, u32[]{:S(2)}) %collective-permute-start) | collective-permute-done | bytes 147488 | tf_op jit(solution)/shard_map/ppermute | solution.py:275
  29.7 0.0 copy-done.3
  29.7 0.3 convolution_bitcast_fusion
  30.1 1.1 %collective-permute-start.1 = (f32[72,128]{1,0:T(8,128)S(1)}, f32[72,128]{1,0:T(8,128)S(1)}, u32[]{:S(2)}, u32[]{:S(2)}) collective-permute-start(f32[72,128]{1,0:T(8,128)S(1)} %get-tuple-element.21), channel_id=1, source_target_pairs={{1,0},{2,1},{3,2},{4,3},{5,4},{6,5},{7,6},{8,7},{9,8},{10,9},{11,1... | collective-permute-start | bytes 110600 | tf_op jit(solution)/shard_map/ppermute | solution.py:226
  31.1 1.3 %collective-permute-start.2 = (f32[72,128]{1,0:T(8,128)S(1)}, f32[72,128]{1,0:T(8,128)S(1)}, u32[]{:S(2)}, u32[]{:S(2)}) collective-permute-start(f32[72,128]{1,0:T(8,128)S(1)} %get-tuple-element.22), channel_id=1, source_target_pairs={{0,1},{1,2},{2,3},{3,4},{4,5},{5,6},{6,7},{7,8},{8,9},{9,10},{10,1... | collective-permute-start | bytes 110600 | tf_op jit(solution)/shard_map/ppermute | solution.py:226
  32.4 0.1 copy.15
  32.5 42.0 %collective-permute-done.1 = f32[72,128]{1,0:T(8,128)S(1)} collective-permute-done((f32[72,128]{1,0:T(8,128)S(1)}, f32[72,128]{1,0:T(8,128)S(1)}, u32[]{:S(2)}, u32[]{:S(2)}) %collective-permute-start.1) | collective-permute-done | bytes 36896 | tf_op jit(solution)/shard_map/ppermute | solution.py:226
  74.5 0.0 collective-permute-done.2
  74.5 0.0 copy-done
  74.5 0.0 copy-done.1
  74.5 0.2 fusion.3.first_step
  74.8 9.7 %all-to-all-done.wire = bf16[32,73,2,128]{3,2,1,0:T(2,128)(2,1)S(1)} async-done(((bf16[32,73,2,128]{3,2,1,0:T(2,128)(2,1)}), bf16[32,73,2,128]{3,2,1,0:T(2,128)(2,1)S(1)}, u32[]{:S(2)}, u32[]{:S(2)}) %all-to-all-start) | async-done | bytes 1196064 | tf_op jit(solution)/shard_map/all_to_all | solution.py:268
  84.5 1.4 %mix.1 = (f32[8,72,128]{2,1,0:T(8,128)S(1)}, f32[72,128]{1,0:T(8,128)S(1)}, f32[72,128]{1,0:T(8,128)S(1)}) custom-call(bf16[32,73,2,128]{3,2,1,0:T(2,128)(2,1)S(1)} %all-to-all-done.wire, f32[8,72,128]{2,1,0:T(8,128)S(1)} %fusion.3.first_step, f32[72,72]{1,0:T(8,128)S(1)} %bitcast.35), custom_call_target="tpu_custom_call" | custom-call | tf_op jit(solution)/shard_map/mix/pallas_call | solution.py:287
  86.0 0.0 collective-permute-start.3
  86.0 1.0 %collective-permute-start.4 = (f32[72,128]{1,0:T(8,128)S(1)}, f32[72,128]{1,0:T(8,128)S(1)}, u32[]{:S(2)}, u32[]{:S(2)}) collective-permute-start(f32[72,128]{1,0:T(8,128)S(1)} %get-tuple-element.20), channel_id=1, source_target_pairs={{1,0},{2,1},{3,2},{4,3},{5,4},{6,5},{7,6},{8,7},{9,8},{10,9},{11,1... | collective-permute-start | bytes 110600 | tf_op jit(solution)/shard_map/ppermute | solution.py:226
  86.9 0.1 copy_bitcast_fusion
  87.1 0.1 copy.27
  87.1 1.0 %direct.1.base = f32[8,72,128]{2,1,0:T(8,128)S(1)} custom-call(bf16[32,73,2,128]{3,2,1,0:T(2,128)(2,1)S(1)} %all-to-all-done.wire, f32[8,72,128]{2,1,0:T(8,128)S(1)} %bitcast.34, f32[8,72,128]{2,1,0:T(8,128)S(1)} %get-tuple-element.18.mixed, f32[8,72,128]{2,1,0:T(8,128)S(1)} %get-tuple-element.24.diag, f32[8,72,128]{2,1,0:T(8,128)S(1)} %get-tuple-element.23.side), custom_call_target="tpu_custom_call" | custom-call | tf_op jit(solution)/shard_map/direct/pallas_call | solution.py:296
  88.1 0.0 collective-permute-done.3.west
  88.1 1.2 %collective-permute-done.4.east = f32[72,128]{1,0:T(8,128)S(1)} collective-permute-done((f32[72,128]{1,0:T(8,128)S(1)}, f32[72,128]{1,0:T(8,128)S(1)}, u32[]{:S(2)}, u32[]{:S(2)}) %collective-permute-start.4) | collective-permute-done | bytes 36896 | tf_op jit(solution)/shard_map/ppermute | solution.py:226
  89.4 1.0 %final.1 = f32[72,8,128]{2,1,0:T(8,128)} custom-call(f32[8,72,128]{2,1,0:T(8,128)S(1)} %direct.1.base, f32[72,128]{1,0:T(8,128)S(1)} %collective-permute-done.3.west, f32[72,128]{1,0:T(8,128)S(1)} %collective-permute-done.4.east, f32[8,72,128]{2,1,0:T(8,128)S(1)} %get-tuple-element.23.side), custom_call_target="tpu_custom_call" | custom-call | tf_op jit(solution)/shard_map/final/pallas_call | solution.py:304
  (1 shorter events, 0.0 us)
Async XLA Ops:
  5.6 16.9 %copy-start.2 = (f32[1,72,8,128]{3,2,1,0:T(8,128)S(1)}, f32[1,72,8,128]{3,2,1,0:T(8,128)}, u32[]{:S(2)}) copy-start(f32[1,72,8,128]{3,2,1,0:T(8,128)} %param.10) | copy-start | bytes 884740
  5.6 24.1 %copy-start.3 = (f32[72,72]{1,0:T(8,128)S(1)}, f32[72,72]{1,0:T(8,128)}, u32[]{:S(2)}) copy-start(f32[72,72]{1,0:T(8,128)} %param.13) | copy-start | bytes 62212
  5.6 68.9 %copy-start = (f32[1,72,8,128]{3,2,1,0:T(8,128)S(1)}, f32[1,72,8,128]{3,2,1,0:T(8,128)}, u32[]{:S(2)}) copy-start(f32[1,72,8,128]{3,2,1,0:T(8,128)} %param.11) | copy-start | bytes 884740
  5.6 68.9 %copy-start.1 = (f32[1,72,8,128]{3,2,1,0:T(8,128)S(1)}, f32[1,72,8,128]{3,2,1,0:T(8,128)}, u32[]{:S(2)}) copy-start(f32[1,72,8,128]{3,2,1,0:T(8,128)} %param.12) | copy-start | bytes 884740
  5.6 78.9 %all-to-all-start = ((bf16[32,73,2,128]{3,2,1,0:T(2,128)(2,1)}), bf16[32,73,2,128]{3,2,1,0:T(2,128)(2,1)S(1)}, u32[]{:S(2)}, u32[]{:S(2)}) async-start(bf16[32,73,2,128]{3,2,1,0:T(2,128)(2,1)} %pack.1), calls=%async_computation | async-start | bytes 2392064 | tf_op jit(solution)/shard_map/all_to_all | solution.py:268
  22.6 7.1 %collective-permute-start = (bf16[8,72,128]{2,1,0:T(8,128)(2,1)S(1)}, bf16[8,72,128]{2,1,0:T(8,128)(2,1)S(1)}, u32[]{:S(2)}, u32[]{:S(2)}) collective-permute-start(bf16[8,72,128]{2,1,0:T(8,128)(2,1)S(1)} %bitcast.36), channel_id=1, source_target_pairs={{32,0},{64,32},{96,64},{128,96},{160,128},{192,160},{224,192},{256... | collective-permute-start | bytes 442376 | tf_op jit(solution)/shard_map/ppermute | solution.py:275
  30.1 44.5 %collective-permute-start.1 = (f32[72,128]{1,0:T(8,128)S(1)}, f32[72,128]{1,0:T(8,128)S(1)}, u32[]{:S(2)}, u32[]{:S(2)}) collective-permute-start(f32[72,128]{1,0:T(8,128)S(1)} %get-tuple-element.21), channel_id=1, source_target_pairs={{1,0},{2,1},{3,2},{4,3},{5,4},{6,5},{7,6},{8,7},{9,8},{10,9},{11,1... | collective-permute-start | bytes 110600 | tf_op jit(solution)/shard_map/ppermute | solution.py:226
  31.1 43.4 %collective-permute-start.2 = (f32[72,128]{1,0:T(8,128)S(1)}, f32[72,128]{1,0:T(8,128)S(1)}, u32[]{:S(2)}, u32[]{:S(2)}) collective-permute-start(f32[72,128]{1,0:T(8,128)S(1)} %get-tuple-element.22), channel_id=1, source_target_pairs={{0,1},{1,2},{2,3},{3,4},{4,5},{5,6},{6,7},{7,8},{8,9},{9,10},{10,1... | collective-permute-start | bytes 110600 | tf_op jit(solution)/shard_map/ppermute | solution.py:226
  86.0 2.2 %collective-permute-start.3 = (f32[72,128]{1,0:T(8,128)S(1)}, f32[72,128]{1,0:T(8,128)S(1)}, u32[]{:S(2)}, u32[]{:S(2)}) collective-permute-start(f32[72,128]{1,0:T(8,128)S(1)} %get-tuple-element.19), channel_id=1, source_target_pairs={{0,1},{1,2},{2,3},{3,4},{4,5},{5,6},{6,7},{7,8},{8,9},{9,10},{10,1... | collective-permute-start | bytes 110600 | tf_op jit(solution)/shard_map/ppermute | solution.py:226
  86.0 3.4 %collective-permute-start.4 = (f32[72,128]{1,0:T(8,128)S(1)}, f32[72,128]{1,0:T(8,128)S(1)}, u32[]{:S(2)}, u32[]{:S(2)}) collective-permute-start(f32[72,128]{1,0:T(8,128)S(1)} %get-tuple-element.20), channel_id=1, source_target_pairs={{1,0},{2,1},{3,2},{4,3},{5,4},{6,5},{7,6},{8,7},{9,8},{10,9},{11,1... | collective-permute-start | bytes 110600 | tf_op jit(solution)/shard_map/ppermute | solution.py:226

commit v4 on v3

--- a/solution.py
+++ b/solution.py
@@ -9,6 +9,7 @@
 LO = 256
 META = 8
 OUT = 8
+PART = 24
 F32 = jnp.float32
 BF16 = jnp.bfloat16
 NT = (((1,), (1,)), ((), ()))
@@ -198,6 +199,7 @@
     lons, width, lats = multiplier.shape
     total = scatter(wire, 0, width)
     lane = lax.broadcasted_iota(jnp.int32, (width, lats), 1)
+    rows = []
     for i in range(lons):
         h, half = i // 2, (i % 2) * CAP
         part = total[h][:, half : half + CAP]
@@ -208,15 +210,25 @@
             beside += mixed[i - 1]
         if i + 1 < lons:
             beside += mixed[i + 1]
-        base[i] = multiplier[i] + part + diag[i] * here + side[i] * beside
-
-
-def final_kernel(base, west, east, side, out):
-    lons = base.shape[0]
-    rows = [base[i] for i in range(lons)]
-    rows[0] += side[0] * west[...]
-    rows[-1] += side[lons - 1] * east[...]
-    out[...] = jnp.stack(rows, axis=1)
+        rows.append(multiplier[i] + part + diag[i] * here + side[i] * beside)
+    base[...] = jnp.stack(rows, axis=1)
+
+
+def final_kernel(base, west, east, side, out_hbm, out, sems):
+    width, lons, lats = base.shape
+    count = width // PART
+    none = [jnp.zeros((PART, lats), F32)] * (lons - 2)
+    stores = []
+    for k in range(count):
+        span = pl.ds(k * PART, PART)
+        first = side[0, span] * west[span]
+        last = side[lons - 1, span] * east[span]
+        out[span] = base[span] + jnp.stack([first] + none + [last], axis=1)
+        store = pltpu.make_async_copy(out.at[span], out_hbm.at[span], sems.at[k])
+        store.start()
+        stores.append(store)
+    for store in stores:
+        store.wait()
 
 
 def halo(first, last):
@@ -295,7 +307,7 @@
     west, east = halo(first, last)
     base = pl.pallas_call(
         direct_kernel,
-        out_shape=field,
+        out_shape=jax.ShapeDtypeStruct((width, lons, lats), F32),
         in_specs=[VMEM] * 5,
         out_specs=VMEM,
         compiler_params=PARAMS,
@@ -305,7 +317,11 @@
         final_kernel,
         out_shape=jax.ShapeDtypeStruct((width, lons, lats), F32),
         in_specs=[VMEM] * 4,
-        out_specs=VMEM,
+        out_specs=HBM,
+        scratch_shapes=[
+            pltpu.VMEM((width, lons, lats), F32),
+            pltpu.SemaphoreType.DMA((width // PART,)),
+        ],
         compiler_params=PARAMS,
         name="final",
     )(base, west, east, side_t)

time: 91.2 us -> 91 us (level)
  no operation moved by 1% of the time
where the time goes in v4:
time: 91 us; the launch traced here: 90.2 us
  waiting for transfers between devices  58.6 us (64%)
  starting transfers between devices  21.5 us (24%)
  Pallas kernels  9.06 us (10%)
    ppermute x4, waiting for transfers between devices, halo(): return (lax.ppermute(last, 'tile', up), lax.ppermute(first, 'tile', down))  43 us
    all_to_all x1, starting transfers between devices, local(): lax.all_to_all(wire, 'tile', split_axis=0, concat_axis=0, tiled=True)  16.9 us
    all_to_all x1, waiting for transfers between devices, local(): lax.all_to_all(wire, 'tile', split_axis=0, concat_axis=0, tiled=True)  9.74 us
    ppermute x1, waiting for transfers between devices, local(): lax.ppermute(mult_t.astype(BF16), 'win', [(i, i - 1) for i in range(1, wi...  5.81 us
    pallas_call x1, Pallas kernels, local(): pl.pallas_call(pack_kernel, out_shape=jax.ShapeDtypeStruct((tiles, width...  5.58 us
    ppermute x4, starting transfers between devices, halo(): return (lax.ppermute(last, 'tile', up), lax.ppermute(first, 'tile', down))  3.33 us
  transfers between devices with their start and end apart: 6, of which 4 were waited for; matrix products, arithmetic and copies ran while one was open for 1% of the time, Pallas kernels for 1%

profile of v4, /device:TPU:1, one launch (start us, length us, event | category | flops | bytes accessed | tf_op | source)
XLA Modules:
  0.0 90.2 jit_solution(9413740981375183540)
XLA Ops:
  0.0 5.6 %pack.1 = bf16[32,73,2,128]{3,2,1,0:T(2,128)(2,1)} custom-call(s32[1,2,1,32]{3,2,1,0:T(1,128)} %counts_hbm.1, bf16[1,2,2048,128]{3,2,1,0:T(8,128)(2,1)} %deps_hbm.1, s32[1,2,1,2048]{3,2,1,0:T(1,128)} %order_hbm.1, s32[1,2,2048]{2,1,0:T(2,128)} %cells_hbm.1, s32[1,2,2048]{2,1,0:T(2,128)} %blocks_hbm.1, bf16[8,72,128]{2,1,0:T(8,128)(2,1)} %jac_hbm.1), custom_call_target="tpu_custom_call" | custom-call | tf_op jit(solution)/shard_map/pack/pallas_call | solution.py:256
  5.6 0.0 copy-start.2
  5.6 0.0 copy-start.3
  5.6 0.0 copy-start
  5.6 0.0 copy-start.1
  5.6 16.9 %all-to-all-start = ((bf16[32,73,2,128]{3,2,1,0:T(2,128)(2,1)}), bf16[32,73,2,128]{3,2,1,0:T(2,128)(2,1)S(1)}, u32[]{:S(2)}, u32[]{:S(2)}) async-start(bf16[32,73,2,128]{3,2,1,0:T(2,128)(2,1)} %pack.1), calls=%async_computation | async-start | bytes 2392064 | tf_op jit(solution)/shard_map/all_to_all | solution.py:280
  22.5 0.0 copy-done.2
  22.5 0.1 copy.28
  22.6 1.3 %collective-permute-start = (bf16[8,72,128]{2,1,0:T(8,128)(2,1)S(1)}, bf16[8,72,128]{2,1,0:T(8,128)(2,1)S(1)}, u32[]{:S(2)}, u32[]{:S(2)}) collective-permute-start(bf16[8,72,128]{2,1,0:T(8,128)(2,1)S(1)} %bitcast.36), channel_id=1, source_target_pairs={{32,0},{64,32},{96,64},{128,96},{160,128},{192,160},{224,192},{256... | collective-permute-start | bytes 442376 | tf_op jit(solution)/shard_map/ppermute | solution.py:287
  23.9 5.8 %collective-permute-done = bf16[8,72,128]{2,1,0:T(8,128)(2,1)S(1)} collective-permute-done((bf16[8,72,128]{2,1,0:T(8,128)(2,1)S(1)}, bf16[8,72,128]{2,1,0:T(8,128)(2,1)S(1)}, u32[]{:S(2)}, u32[]{:S(2)}) %collective-permute-start) | collective-permute-done | bytes 147488 | tf_op jit(solution)/shard_map/ppermute | solution.py:287
  29.7 0.0 copy-done.3
  29.7 0.3 convolution_bitcast_fusion
  30.1 1.1 %collective-permute-start.1 = (f32[72,128]{1,0:T(8,128)S(1)}, f32[72,128]{1,0:T(8,128)S(1)}, u32[]{:S(2)}, u32[]{:S(2)}) collective-permute-start(f32[72,128]{1,0:T(8,128)S(1)} %get-tuple-element.21), channel_id=1, source_target_pairs={{1,0},{2,1},{3,2},{4,3},{5,4},{6,5},{7,6},{8,7},{9,8},{10,9},{11,1... | collective-permute-start | bytes 110600 | tf_op jit(solution)/shard_map/ppermute | solution.py:238
  31.1 1.3 %collective-permute-start.2 = (f32[72,128]{1,0:T(8,128)S(1)}, f32[72,128]{1,0:T(8,128)S(1)}, u32[]{:S(2)}, u32[]{:S(2)}) collective-permute-start(f32[72,128]{1,0:T(8,128)S(1)} %get-tuple-element.22), channel_id=1, source_target_pairs={{0,1},{1,2},{2,3},{3,4},{4,5},{5,6},{6,7},{7,8},{8,9},{9,10},{10,1... | collective-permute-start | bytes 110600 | tf_op jit(solution)/shard_map/ppermute | solution.py:238
  32.4 0.1 copy.15
  32.5 42.0 %collective-permute-done.1 = f32[72,128]{1,0:T(8,128)S(1)} collective-permute-done((f32[72,128]{1,0:T(8,128)S(1)}, f32[72,128]{1,0:T(8,128)S(1)}, u32[]{:S(2)}, u32[]{:S(2)}) %collective-permute-start.1) | collective-permute-done | bytes 36896 | tf_op jit(solution)/shard_map/ppermute | solution.py:238
  74.5 0.0 collective-permute-done.2
  74.5 0.0 copy-done
  74.5 0.0 copy-done.1
  74.5 0.2 fusion.3.first_step
  74.8 9.7 %all-to-all-done.wire = bf16[32,73,2,128]{3,2,1,0:T(2,128)(2,1)S(1)} async-done(((bf16[32,73,2,128]{3,2,1,0:T(2,128)(2,1)}), bf16[32,73,2,128]{3,2,1,0:T(2,128)(2,1)S(1)}, u32[]{:S(2)}, u32[]{:S(2)}) %all-to-all-start) | async-done | bytes 1196064 | tf_op jit(solution)/shard_map/all_to_all | solution.py:280
  84.5 1.4 %mix.1 = (f32[8,72,128]{2,1,0:T(8,128)S(1)}, f32[72,128]{1,0:T(8,128)S(1)}, f32[72,128]{1,0:T(8,128)S(1)}) custom-call(bf16[32,73,2,128]{3,2,1,0:T(2,128)(2,1)S(1)} %all-to-all-done.wire, f32[8,72,128]{2,1,0:T(8,128)S(1)} %fusion.3.first_step, f32[72,72]{1,0:T(8,128)S(1)} %bitcast.35), custom_call_target="tpu_custom_call" | custom-call | tf_op jit(solution)/shard_map/mix/pallas_call | solution.py:299
  86.0 0.0 collective-permute-start.3
  86.0 1.0 %collective-permute-start.4 = (f32[72,128]{1,0:T(8,128)S(1)}, f32[72,128]{1,0:T(8,128)S(1)}, u32[]{:S(2)}, u32[]{:S(2)}) collective-permute-start(f32[72,128]{1,0:T(8,128)S(1)} %get-tuple-element.20), channel_id=1, source_target_pairs={{1,0},{2,1},{3,2},{4,3},{5,4},{6,5},{7,6},{8,7},{9,8},{10,9},{11,1... | collective-permute-start | bytes 110600 | tf_op jit(solution)/shard_map/ppermute | solution.py:238
  86.9 0.1 copy_bitcast_fusion
  87.1 0.1 copy.27
  87.1 1.3 %direct.1.base = f32[72,8,128]{2,1,0:T(8,128)S(1)} custom-call(bf16[32,73,2,128]{3,2,1,0:T(2,128)(2,1)S(1)} %all-to-all-done.wire, f32[8,72,128]{2,1,0:T(8,128)S(1)} %bitcast.34, f32[8,72,128]{2,1,0:T(8,128)S(1)} %get-tuple-element.18.mixed, f32[8,72,128]{2,1,0:T(8,128)S(1)} %get-tuple-element.24.diag, f32[8,72,128]{2,1,0:T(8,128)S(1)} %get-tuple-element.23.side), custom_call_target="tpu_custom_call" | custom-call | tf_op jit(solution)/shard_map/direct/pallas_call | solution.py:308
  88.4 0.0 collective-permute-done.3.west
  88.4 1.0 %collective-permute-done.4.east = f32[72,128]{1,0:T(8,128)S(1)} collective-permute-done((f32[72,128]{1,0:T(8,128)S(1)}, f32[72,128]{1,0:T(8,128)S(1)}, u32[]{:S(2)}, u32[]{:S(2)}) %collective-permute-start.4) | collective-permute-done | bytes 36896 | tf_op jit(solution)/shard_map/ppermute | solution.py:238
  89.4 0.8 final.1
  (1 shorter events, 0.0 us)
Async XLA Ops:
  5.6 16.9 %copy-start.2 = (f32[1,72,8,128]{3,2,1,0:T(8,128)S(1)}, f32[1,72,8,128]{3,2,1,0:T(8,128)}, u32[]{:S(2)}) copy-start(f32[1,72,8,128]{3,2,1,0:T(8,128)} %param.10) | copy-start | bytes 884740
  5.6 24.1 %copy-start.3 = (f32[72,72]{1,0:T(8,128)S(1)}, f32[72,72]{1,0:T(8,128)}, u32[]{:S(2)}) copy-start(f32[72,72]{1,0:T(8,128)} %param.13) | copy-start | bytes 62212
  5.6 68.9 %copy-start = (f32[1,72,8,128]{3,2,1,0:T(8,128)S(1)}, f32[1,72,8,128]{3,2,1,0:T(8,128)}, u32[]{:S(2)}) copy-start(f32[1,72,8,128]{3,2,1,0:T(8,128)} %param.11) | copy-start | bytes 884740
  5.6 68.9 %copy-start.1 = (f32[1,72,8,128]{3,2,1,0:T(8,128)S(1)}, f32[1,72,8,128]{3,2,1,0:T(8,128)}, u32[]{:S(2)}) copy-start(f32[1,72,8,128]{3,2,1,0:T(8,128)} %param.12) | copy-start | bytes 884740
  5.6 78.9 %all-to-all-start = ((bf16[32,73,2,128]{3,2,1,0:T(2,128)(2,1)}), bf16[32,73,2,128]{3,2,1,0:T(2,128)(2,1)S(1)}, u32[]{:S(2)}, u32[]{:S(2)}) async-start(bf16[32,73,2,128]{3,2,1,0:T(2,128)(2,1)} %pack.1), calls=%async_computation | async-start | bytes 2392064 | tf_op jit(solution)/shard_map/all_to_all | solution.py:280
  22.6 7.1 %collective-permute-start = (bf16[8,72,128]{2,1,0:T(8,128)(2,1)S(1)}, bf16[8,72,128]{2,1,0:T(8,128)(2,1)S(1)}, u32[]{:S(2)}, u32[]{:S(2)}) collective-permute-start(bf16[8,72,128]{2,1,0:T(8,128)(2,1)S(1)} %bitcast.36), channel_id=1, source_target_pairs={{32,0},{64,32},{96,64},{128,96},{160,128},{192,160},{224,192},{256... | collective-permute-start | bytes 442376 | tf_op jit(solution)/shard_map/ppermute | solution.py:287
  30.1 44.5 %collective-permute-start.1 = (f32[72,128]{1,0:T(8,128)S(1)}, f32[72,128]{1,0:T(8,128)S(1)}, u32[]{:S(2)}, u32[]{:S(2)}) collective-permute-start(f32[72,128]{1,0:T(8,128)S(1)} %get-tuple-element.21), channel_id=1, source_target_pairs={{1,0},{2,1},{3,2},{4,3},{5,4},{6,5},{7,6},{8,7},{9,8},{10,9},{11,1... | collective-permute-start | bytes 110600 | tf_op jit(solution)/shard_map/ppermute | solution.py:238
  31.1 43.4 %collective-permute-start.2 = (f32[72,128]{1,0:T(8,128)S(1)}, f32[72,128]{1,0:T(8,128)S(1)}, u32[]{:S(2)}, u32[]{:S(2)}) collective-permute-start(f32[72,128]{1,0:T(8,128)S(1)} %get-tuple-element.22), channel_id=1, source_target_pairs={{0,1},{1,2},{2,3},{3,4},{4,5},{5,6},{6,7},{7,8},{8,9},{9,10},{10,1... | collective-permute-start | bytes 110600 | tf_op jit(solution)/shard_map/ppermute | solution.py:238
  86.0 2.4 %collective-permute-start.3 = (f32[72,128]{1,0:T(8,128)S(1)}, f32[72,128]{1,0:T(8,128)S(1)}, u32[]{:S(2)}, u32[]{:S(2)}) collective-permute-start(f32[72,128]{1,0:T(8,128)S(1)} %get-tuple-element.19), channel_id=1, source_target_pairs={{0,1},{1,2},{2,3},{3,4},{4,5},{5,6},{6,7},{7,8},{8,9},{9,10},{10,1... | collective-permute-start | bytes 110600 | tf_op jit(solution)/shard_map/ppermute | solution.py:238
  86.0 3.4 %collective-permute-start.4 = (f32[72,128]{1,0:T(8,128)S(1)}, f32[72,128]{1,0:T(8,128)S(1)}, u32[]{:S(2)}, u32[]{:S(2)}) collective-permute-start(f32[72,128]{1,0:T(8,128)S(1)} %get-tuple-element.20), channel_id=1, source_target_pairs={{1,0},{2,1},{3,2},{4,3},{5,4},{6,5},{7,6},{8,7},{9,8},{10,9},{11,1... | collective-permute-start | bytes 110600 | tf_op jit(solution)/shard_map/ppermute | solution.py:238
